TPU v7x, 32 devices: a whole 2x2x4 slice. The times are simulated.
32 devices in a mesh: leaf: 8 (over y, x, core), col: 4 (over z).
Axes of the slice: x: 2, y: 2, z: 4, core: 2. Of those that a mesh axis runs over, the one named last changes fastest.
Arguments:
- right_side: float32 [31, 2560, 256], P(None, 'leaf'), may hold values from -6 to 6
- reciprocal_pivot_matrix: bfloat16 [31, 2560, 2560], P(None, 'col', 'leaf'), as said below
- panels: bfloat16 [98, 2560, 2560], P(None, 'leaf', 'col'), may hold values from -0.03125 to 0.03125
- parent: int32 [31], replicated, may hold values from 16 to 30, as said below
Outputs:
- solution: float32 [31, 2560, 256], P(None, 'leaf')
Inputs may be any that keep to these rules, and one draw needn't show every extreme that they name: Supernodes 0 to 15 have parents among 16 to 23, 16 to 23 among 24 to 27, 24 to 27 among 28 and 29, 28 and 29 have parent 30, and entry 30 is 30 itself; each supernode of levels 1 to 4 is the parent of exactly two supernodes of the level below. `reciprocal_pivot_matrix`: each block is lower triangular with a positive diagonal.
All inputs are finite; a program needn't handle non-finite values.
Results may differ from a plain program's by a relative error of at most 0.03.
Values may be sent and summed in bfloat16 or wider, within the bound.
A program may use at most 192 MiB of HBM per device.

v0:
```python
import jax
import jax.numpy as jnp
import numpy as np
from jax import lax
from jax.sharding import PartitionSpec as P

level_starts = (0, 16, 24, 28, 30)
level_counts = (16, 8, 4, 2, 1)


def pair_table():
    sources = []
    distances = []
    for tree_level in range(5):
        for tree_vertex in range(
            level_starts[tree_level], level_starts[tree_level] + level_counts[tree_level]
        ):
            for distance in range(1, 5 - tree_level):
                sources.append(tree_vertex)
                distances.append(distance)
    return (sources, distances)


def node_level(tree_vertex):
    deepest = 0
    for tree_level in range(5):
        if level_starts[tree_level] <= tree_vertex:
            deepest = tree_level
    return deepest


def pair_offset(tree_level):
    initial_position = 0
    for lower in range(tree_level):
        initial_position = initial_position + level_counts[lower] * (4 - lower)
    return initial_position


def pair_ancestors(parent):
    sources, distances = pair_table()
    climbed = [jnp.arange(parent.shape[0], dtype=jnp.int32)]
    for distance in range(4):
        climbed.append(parent[climbed[-1]])
    return jnp.stack(
        [climbed[distance][source_node] for source_node, distance in zip(sources, distances)]
    )


def forward_products(panel_local, forward_stack, ancestor, pair_list, start_node, node_count):
    sources, distances = pair_table()
    chosen = np.array(pair_list, dtype=np.int32)
    feeders = np.array([sources[node_pairing] for node_pairing in pair_list], dtype=np.int32)
    products = jnp.einsum(
        "sjv,svk->sjk",
        panel_local[chosen],
        forward_stack[feeders],
        preferred_element_type=jnp.float32,
    )
    slots = jnp.arange(node_count, dtype=jnp.int32) + start_node
    onehot = (slots[:, None] == ancestor[chosen][None, :]).astype(jnp.float32)
    return jnp.einsum("kp,par->kar", onehot, products, precision=lax.Precision.HIGHEST)


def solve(right_side, diag_local, panel_local, ancestor):
    sources, distances = pair_table()
    node_total = right_side.shape[0]
    load_vector_count = right_side.shape[2]
    col_rows = diag_local.shape[1]
    leaf_rows = diag_local.shape[2]
    forward_stack = jnp.zeros((node_total, col_rows, load_vector_count), jnp.bfloat16)
    forward_levels = [None] * 5
    for tree_level in range(5):
        start_node = level_starts[tree_level]
        node_count = level_counts[tree_level]
        reduced = right_side[start_node : start_node + node_count]
        if tree_level > 0:
            arriving = [
                node_pairing
                for node_pairing in range(len(sources))
                if node_level(sources[node_pairing]) + distances[node_pairing] == tree_level
            ]
            partial_value = forward_products(
                panel_local, forward_stack, ancestor, arriving, start_node, node_count
            )
            reduced = reduced - lax.psum(partial_value.astype(jnp.bfloat16), "col").astype(
                jnp.float32
            )
        division_count = jnp.einsum(
            "kcl,klr->kcr",
            diag_local[start_node : start_node + node_count],
            reduced.astype(jnp.bfloat16),
            preferred_element_type=jnp.float32,
        )
        forward_value = lax.psum(division_count.astype(jnp.bfloat16), "leaf").astype(jnp.float32)
        forward_levels[tree_level] = forward_value
        forward_stack = forward_stack.at[start_node : start_node + node_count].set(
            forward_value.astype(jnp.bfloat16)
        )
    solution_stack = jnp.zeros((node_total, leaf_rows, load_vector_count), jnp.bfloat16)
    results = [None] * 5
    for tree_level in (4, 3, 2, 1, 0):
        start_node = level_starts[tree_level]
        node_count = level_counts[tree_level]
        corrected = forward_levels[tree_level]
        if tree_level < 4:
            initial_position = pair_offset(tree_level)
            span_pairs = node_count * (4 - tree_level)
            upper_node = solution_stack[ancestor[initial_position : initial_position + span_pairs]]
            products = jnp.einsum(
                "boj,boh->bjh",
                panel_local[initial_position : initial_position + span_pairs],
                upper_node,
                preferred_element_type=jnp.float32,
            )
            partial_value = jnp.sum(
                products.reshape(node_count, 4 - tree_level, col_rows, load_vector_count), axis=1
            )
            corrected = corrected - lax.psum(partial_value.astype(jnp.bfloat16), "leaf").astype(
                jnp.float32
            )
        division_count = jnp.einsum(
            "kcl,kcr->klr",
            diag_local[start_node : start_node + node_count],
            corrected.astype(jnp.bfloat16),
            preferred_element_type=jnp.float32,
        )
        solution = lax.psum(division_count.astype(jnp.bfloat16), "col").astype(jnp.float32)
        results[tree_level] = solution
        solution_stack = solution_stack.at[start_node : start_node + node_count].set(
            solution.astype(jnp.bfloat16)
        )
    return jnp.concatenate(results, axis=0)


def shards(right_side, reciprocal_pivot_matrix, panels, parent):
    ancestor = pair_ancestors(parent)
    return solve(right_side, reciprocal_pivot_matrix, panels, ancestor)


def solution(mesh):
    return jax.shard_map(
        shards,
        mesh=mesh,
        in_specs=(P(None, "leaf", None), P(None, "col", "leaf"), P(None, "leaf", "col"), P()),
        out_specs=P(None, "leaf", None),
        check_vma=False,
    )
```

profile of v0, /device:TPU:0, one launch (start us, length us, event | category | flops | bytes accessed | tf_op | source)
XLA Modules:
  0.0 1331.2 jit_solution(3711821767542379602)
XLA Ops:
  6.5 9.9 convolution_convert_fusion
  24.0 61.1 %stack.204 = s32[98]{0:T(128)S(1)} concatenate(s32[1]{0:T(128)} %get-tuple-element.201, s32[1]{0:T(128)} %get-tuple-element.184, s32[1]{0:T(128)} %get-tuple-element.198, s32[1]{0:T(128)} %get-tuple-element.175, s32[1]{0:T(128)} %get-tuple-element.202, s32[1]{0:T(128)} %get-tuple-element.183, s32[1]{0:T(128)} %get-tuple-element.197, s32[1]{0:T(128)} %get-tuple-element.174, ...), dimensions={0} | concatenate | bytes 784 | tf_op jit(solution)/shard_map/stack | solution.py:44
  85.8 7.4 gather_fusion.7
  93.2 18.7 %all-reduce.21.cloned.1.call-done = bf16[16,640,256]{2,1,0:T(8,128)(2,1)} async-done(((bf16[16,640,256]{2,1,0:T(8,128)(2,1)}), bf16[16,640,256]{2,1,0:T(8,128)(2,1)}) %all-reduce.21.cloned.1.call-update) | async-done | bytes 5242896 | tf_op jit(solution)/shard_map/psum | solution.py:94
  111.9 7.5 scatter.26
  119.4 7.1 gather_fusion.8
  126.5 6.6 fusion.100
  133.1 6.1 fusion.30
  139.7 59.7 %all-reduce.23.cloned.1.call-done = bf16[8,320,256]{2,0,1:T(8,128)(2,1)} async-done(((bf16[8,320,256]{2,0,1:T(8,128)(2,1)}), bf16[8,320,256]{2,0,1:T(8,128)(2,1)}) %all-reduce.23.cloned.1.call-update) | async-done | bytes 1310736 | tf_op jit(solution)/shard_map/psum | solution.py:85
  199.4 2.8 fusion.22
  202.2 5.2 convert_bitcast_fusion.1
  208.2 10.0 gather_fusion.10
  218.2 53.6 %all-reduce.25.cloned.1.call-done = bf16[8,640,256]{2,1,0:T(8,128)(2,1)} async-done(((bf16[8,640,256]{2,1,0:T(8,128)(2,1)}), bf16[8,640,256]{2,1,0:T(8,128)(2,1)}) %all-reduce.25.cloned.1.call-update) | async-done | bytes 2621456 | tf_op jit(solution)/shard_map/psum | solution.py:94
  271.9 3.4 constant_dynamic-update-slice_fusion.10
  275.3 9.0 gather_fusion.11
  284.3 8.2 fusion.101
  292.5 7.9 fusion.47
  300.7 40.0 %all-reduce.27.cloned.1.call-done = bf16[4,320,256]{2,0,1:T(4,128)(2,1)} async-done(((bf16[4,320,256]{2,0,1:T(4,128)(2,1)}), bf16[4,320,256]{2,0,1:T(4,128)(2,1)}) %all-reduce.27.cloned.1.call-update) | async-done | bytes 655376 | tf_op jit(solution)/shard_map/psum | solution.py:85
  342.9 3.5 fusion.38
  347.2 10.2 gather_fusion.13
  357.4 46.3 %all-reduce.29.cloned.1.call-done = bf16[4,640,256]{2,1,0:T(8,128)(2,1)} async-done(((bf16[4,640,256]{2,1,0:T(8,128)(2,1)}), bf16[4,640,256]{2,1,0:T(8,128)(2,1)}) %all-reduce.29.cloned.1.call-update) | async-done | bytes 1310736 | tf_op jit(solution)/shard_map/psum | solution.py:94
  403.7 2.5 constant_dynamic-update-slice_fusion.9
  406.2 9.4 gather_fusion.14
  415.6 9.3 fusion.102
  424.8 8.6 fusion.4
  434.3 35.6 %all-reduce.31.cloned.1.call-done = bf16[2,320,256]{2,1,0:T(8,128)(2,1)} async-done(((bf16[2,320,256]{2,1,0:T(8,128)(2,1)}), bf16[2,320,256]{2,1,0:T(8,128)(2,1)}) %all-reduce.31.cloned.1.call-update) | async-done | bytes 327696 | tf_op jit(solution)/shard_map/psum | solution.py:85
  469.9 2.9 fusion.52
  473.5 10.3 gather_fusion.5
  483.9 44.0 %all-reduce.33.cloned.1.call-done = bf16[2,640,256]{2,1,0:T(8,128)(2,1)} async-done(((bf16[2,640,256]{2,1,0:T(8,128)(2,1)}), bf16[2,640,256]{2,1,0:T(8,128)(2,1)}) %all-reduce.33.cloned.1.call-update) | async-done | bytes 655376 | tf_op jit(solution)/shard_map/psum | solution.py:94
  529.9 10.0 gather_fusion.15
  539.8 15.1 %fusion.103 = f32[30,320,256]{2,1,0:T(8,128)} fusion(bf16[30,320,640]{2,1,0:T(8,128)(2,1)} %gather_fusion.5, bf16[30,640,256]{2,1,0:T(8,128)(2,1)} %gather_fusion.15), kind=kOutput, calls=%fused_computation.160 | convolution fusion | flops 3145728000 | bytes 31948800 | tf_op jit(solution)/shard_map/sjv,svk->sjk/dot_general | solution.py:53
  555.0 12.8 fusion.2
  568.5 34.1 %all-reduce.35.cloned.1.call-done = bf16[1,320,256]{2,1,0:T(8,128)(2,1)} async-done(((bf16[1,320,256]{2,1,0:T(8,128)(2,1)}), bf16[1,320,256]{2,1,0:T(8,128)(2,1)}) %all-reduce.35.cloned.1.call-update) | async-done | bytes 163856 | tf_op jit(solution)/shard_map/psum | solution.py:85
  602.6 2.3 fusion.57
  605.0 54.3 %all-reduce.37.cloned.1.call-done = bf16[640,256]{0,1:T(8,128)(2,1)} async-done(((bf16[640,256]{0,1:T(8,128)(2,1)}), bf16[640,256]{0,1:T(8,128)(2,1)}) %all-reduce.37.cloned.1.call-update) | async-done | bytes 327696 | tf_op jit(solution)/shard_map/psum | solution.py:94
  661.5 34.2 %all-reduce.39.cloned.1.call-done = bf16[1,320,256]{2,1,0:T(8,128)(2,1)} async-done(((bf16[1,320,256]{2,1,0:T(8,128)(2,1)}), bf16[1,320,256]{2,1,0:T(8,128)(2,1)}) %all-reduce.39.cloned.1.call-update) | async-done | bytes 163856 | tf_op jit(solution)/shard_map/psum | solution.py:127
  695.7 3.8 scatter.34
  699.4 3.0 gather_fusion.16
  702.5 2.6 fusion.53
  705.1 4.8 stack.213
  709.9 50.1 %all-reduce.41.cloned.1.call-done = bf16[2,640,256]{2,1,0:T(8,128)(2,1)} async-done(((bf16[2,640,256]{2,1,0:T(8,128)(2,1)}), bf16[2,640,256]{2,1,0:T(8,128)(2,1)}) %all-reduce.41.cloned.1.call-update) | async-done | bytes 655376 | tf_op jit(solution)/shard_map/psum | solution.py:118
  760.0 2.6 fusion.58
  762.7 35.6 %all-reduce.43.cloned.1.call-done = bf16[2,320,256]{2,1,0:T(8,128)(2,1)} async-done(((bf16[2,320,256]{2,1,0:T(8,128)(2,1)}), bf16[2,320,256]{2,1,0:T(8,128)(2,1)}) %all-reduce.43.cloned.1.call-update) | async-done | bytes 327696 | tf_op jit(solution)/shard_map/psum | solution.py:127
  800.0 4.1 gather_fusion.17
  804.2 4.3 bitcast_reduce_fusion.1
  810.0 57.6 %all-reduce.45.cloned.1.call-done = bf16[4,640,256]{2,1,0:T(8,128)(2,1)} async-done(((bf16[4,640,256]{2,1,0:T(8,128)(2,1)}), bf16[4,640,256]{2,1,0:T(8,128)(2,1)}) %all-reduce.45.cloned.1.call-update) | async-done | bytes 1310736 | tf_op jit(solution)/shard_map/psum | solution.py:118
  867.6 3.4 fusion.54
  871.1 15.3 %stack.238 = s32[24,1]{0,1:T(1,128)S(1)} concatenate(s32[1,1]{0,1:T(1,128)} %bitcast.34, s32[1,1]{0,1:T(1,128)} %bitcast.35, s32[1,1]{0,1:T(1,128)} %bitcast.36, s32[1,1]{0,1:T(1,128)} %bitcast.37, s32[1,1]{0,1:T(1,128)} %bitcast.38, s32[1,1]{0,1:T(1,128)} %bitcast.39, s32[1,1]{0,1:T(1,128)} %bitcast.40, s32[1,1]{0,1:T(1,128)} %bitcast.41, s32[1,1]{0,1:T(1,128)} %bitcast.42, ...), dimensions={0} | concatenate | bytes 192 | tf_op jit(solution)/shard_map/stack | solution.py:44
  886.4 24.5 %all-reduce.47.cloned.1.call-done = bf16[4,320,256]{2,1,0:T(8,128)(2,1)} async-done(((bf16[4,320,256]{2,1,0:T(8,128)(2,1)}), bf16[4,320,256]{2,1,0:T(8,128)(2,1)}) %all-reduce.47.cloned.1.call-update) | async-done | bytes 655376 | tf_op jit(solution)/shard_map/psum | solution.py:127
  912.9 5.3 gather_fusion.18
  918.1 12.9 fusion.6
  931.1 6.9 reduce_sum.32
  937.9 2.6 copy.60
  940.6 64.2 %all-reduce.49.cloned.1.call-done = bf16[8,640,256]{2,1,0:T(8,128)(2,1)} async-done(((bf16[8,640,256]{2,1,0:T(8,128)(2,1)}), bf16[8,640,256]{2,1,0:T(8,128)(2,1)}) %all-reduce.49.cloned.1.call-update) | async-done | bytes 2621456 | tf_op jit(solution)/shard_map/psum | solution.py:118
  1004.9 5.8 fusion.41
  1012.1 58.4 %all-reduce.51.cloned.1.call-done = bf16[8,320,256]{2,1,0:T(8,128)(2,1)} async-done(((bf16[8,320,256]{2,1,0:T(8,128)(2,1)}), bf16[8,320,256]{2,1,0:T(8,128)(2,1)}) %all-reduce.51.cloned.1.call-update) | async-done | bytes 1310736 | tf_op jit(solution)/shard_map/psum | solution.py:127
  1070.4 2.5 constant_dynamic-update-slice_fusion.5
  1072.9 8.8 gather_fusion.19
  1081.7 20.7 %bitcast_reduce_fusion = bf16[16,640,256]{1,2,0:T(8,128)(2,1)} fusion(bf16[64,320,256]{2,1,0:T(8,128)(2,1)} %gather_fusion.19, bf16[98,320,640]{2,1,0:T(8,128)(2,1)} %param.42), kind=kOutput, calls=%fused_computation.20 | convolution fusion | flops 6718750720 | bytes 41943040 | tf_op jit(solution)/shard_map/boj,boh->bjh/dot_general | solution.py:109
  1102.3 7.8 copy.61
  1110.2 92.4 %all-reduce.53.cloned.1.call-done = bf16[16,640,256]{2,1,0:T(8,128)(2,1)} async-done(((bf16[16,640,256]{2,1,0:T(8,128)(2,1)}), bf16[16,640,256]{2,1,0:T(8,128)(2,1)}) %all-reduce.53.cloned.1.call-update) | async-done | bytes 5242896 | tf_op jit(solution)/shard_map/psum | solution.py:118
  1202.6 9.7 convert_bitcast_fusion
  1212.3 104.3 %all-reduce.55.cloned.1.call-done = bf16[16,320,256]{2,1,0:T(8,128)(2,1)} async-done(((bf16[16,320,256]{2,1,0:T(8,128)(2,1)}), bf16[16,320,256]{2,1,0:T(8,128)(2,1)}) %all-reduce.55.cloned.1.call-update) | async-done | bytes 2621456 | tf_op jit(solution)/shard_map/psum | solution.py:127
  1318.8 5.3 concatenate.84
  (121 shorter events, 28.2 us)
Async XLA Ops:
  6.5 10.2 copy-start
  6.5 105.4 %all-reduce.21.cloned.1.call-start = ((), (), s32[]{:S(2)}) async-start(), calls=%async_computation | async-start | bytes 10485760 | tf_op jit(solution)/shard_map/psum | solution.py:94
  16.4 183.0 %all-reduce.23.cloned.1.call-start = ((), (), s32[]{:S(2)}) async-start(), calls=%async_computation.1 | async-start | bytes 2621440 | tf_op jit(solution)/shard_map/psum | solution.py:85
  133.1 66.4 %slice-start = ((f32[31,320,256]{2,1,0:T(8,128)}), f32[8,320,256]{2,1,0:T(8,128)S(1)}, s32[]{:S(2)}) async-start(f32[31,320,256]{2,1,0:T(8,128)} %param.40), calls=%async_computation.18 | async-start | bytes 5242880 | tf_op jit(solution)/shard_map/slice | solution.py:75
  139.2 132.7 %all-reduce.25.cloned.1.call-start = ((), (), s32[]{:S(2)}) async-start(), calls=%async_computation.2 | async-start | bytes 5242880 | tf_op jit(solution)/shard_map/psum | solution.py:94
  202.2 5.3 copy-start.10
  207.4 133.3 %all-reduce.27.cloned.1.call-start = ((), (), s32[]{:S(2)}) async-start(), calls=%async_computation.3 | async-start | bytes 1310720 | tf_op jit(solution)/shard_map/psum | solution.py:85
  292.5 48.3 %slice-start.1 = ((f32[31,320,256]{2,1,0:T(8,128)}), f32[4,320,256]{2,1,0:T(8,128)S(1)}, s32[]{:S(2)}) async-start(f32[31,320,256]{2,1,0:T(8,128)} %param.40), calls=%async_computation.19 | async-start | bytes 2621440 | tf_op jit(solution)/shard_map/slice | solution.py:75
  300.4 46.0 %copy-start.9 = (s32[28]{0:T(128)S(1)}, s32[28]{0:T(128)}, u32[]{:S(2)}) copy-start(s32[28]{0:T(128)} %constant.267) | copy-start | bytes 340
  300.5 103.3 %all-reduce.29.cloned.1.call-start = ((), (), s32[]{:S(2)}) async-start(), calls=%async_computation.4 | async-start | bytes 2621440 | tf_op jit(solution)/shard_map/psum | solution.py:94
  346.4 123.5 %all-reduce.31.cloned.1.call-start = ((), (), s32[]{:S(2)}) async-start(), calls=%async_computation.5 | async-start | bytes 655360 | tf_op jit(solution)/shard_map/psum | solution.py:85
  424.8 48.0 %copy-start.8 = (s32[30]{0:T(128)S(1)}, s32[30]{0:T(128)}, u32[]{:S(2)}) copy-start(s32[30]{0:T(128)} %constant.263) | copy-start | bytes 364
  434.3 93.6 %all-reduce.33.cloned.1.call-start = ((), (), s32[]{:S(2)}) async-start(), calls=%async_computation.6 | async-start | bytes 1310720 | tf_op jit(solution)/shard_map/psum | solution.py:94
  472.8 129.9 %all-reduce.35.cloned.1.call-start = ((), (), s32[]{:S(2)}) async-start(), calls=%async_computation.7 | async-start | bytes 327680 | tf_op jit(solution)/shard_map/psum | solution.py:85
  568.5 191.5 %copy-start.7 = (bf16[2,640,256]{2,1,0:T(8,128)(2,1)S(1)}, bf16[2,640,256]{2,1,0:T(8,128)(2,1)}, u32[]{:S(2)}) copy-start(bf16[2,640,256]{2,1,0:T(8,128)(2,1)} %all-reduce.33.cloned.1.call-done) | copy-start | bytes 1966084
  568.5 90.8 %all-reduce.37.cloned.1.call-start = ((), (), s32[]{:S(2)}) async-start(), calls=%async_computation.8 | async-start | bytes 655360 | tf_op jit(solution)/shard_map/psum | solution.py:94
  604.9 90.7 %all-reduce.39.cloned.1.call-start = ((), (), s32[]{:S(2)}) async-start(), calls=%async_computation.9 | async-start | bytes 327680 | tf_op jit(solution)/shard_map/psum | solution.py:127
  661.5 98.6 %all-reduce.41.cloned.1.call-start = ((), (), s32[]{:S(2)}) async-start(), calls=%async_computation.10 | async-start | bytes 1310720 | tf_op jit(solution)/shard_map/psum | solution.py:118
  705.1 93.2 %all-reduce.43.cloned.1.call-start = ((), (), s32[]{:S(2)}) async-start(), calls=%async_computation.11 | async-start | bytes 655360 | tf_op jit(solution)/shard_map/psum | solution.py:127
  762.6 105.0 %all-reduce.45.cloned.1.call-start = ((), (), s32[]{:S(2)}) async-start(), calls=%async_computation.12 | async-start | bytes 2621440 | tf_op jit(solution)/shard_map/psum | solution.py:118
  804.2 63.4 %copy-start.4 = (bf16[4,640,256]{2,1,0:T(8,128)(2,1)S(1)}, bf16[4,640,256]{2,1,0:T(8,128)(2,1)}, u32[]{:S(2)}) copy-start(bf16[4,640,256]{2,1,0:T(8,128)(2,1)} %all-reduce.29.cloned.1.call-done) | copy-start | bytes 3932164
  809.9 101.0 %all-reduce.47.cloned.1.call-start = ((), (), s32[]{:S(2)}) async-start(), calls=%async_computation.13 | async-start | bytes 1310720 | tf_op jit(solution)/shard_map/psum | solution.py:127
  871.0 133.8 %all-reduce.49.cloned.1.call-start = ((), (), s32[]{:S(2)}) async-start(), calls=%async_computation.14 | async-start | bytes 5242880 | tf_op jit(solution)/shard_map/psum | solution.py:118
  940.6 129.8 %all-reduce.51.cloned.1.call-start = ((), (), s32[]{:S(2)}) async-start(), calls=%async_computation.15 | async-start | bytes 2621440 | tf_op jit(solution)/shard_map/psum | solution.py:127
  1010.7 191.9 %all-reduce.53.cloned.1.call-start = ((), (), s32[]{:S(2)}) async-start(), calls=%async_computation.16 | async-start | bytes 10485760 | tf_op jit(solution)/shard_map/psum | solution.py:118
  1110.2 206.5 %all-reduce.55.cloned.1.call-start = ((), (), s32[]{:S(2)}) async-start(), calls=%async_computation.17 | async-start | bytes 5242880 | tf_op jit(solution)/shard_map/psum | solution.py:127
  1212.3 106.3 %copy-start.2 = (bf16[8,320,256]{2,1,0:T(8,128)(2,1)S(1)}, bf16[8,320,256]{2,1,0:T(8,128)(2,1)}, u32[]{:S(2)}) copy-start(bf16[8,320,256]{2,1,0:T(8,128)(2,1)} %all-reduce.51.cloned.1.call-done) | copy-start | bytes 3932164
  1212.3 106.4 %copy-start.3 = (bf16[4,320,256]{2,1,0:T(8,128)(2,1)S(1)}, bf16[4,320,256]{2,1,0:T(8,128)(2,1)}, u32[]{:S(2)}) copy-start(bf16[4,320,256]{2,1,0:T(8,128)(2,1)} %all-reduce.47.cloned.1.call-done) | copy-start | bytes 1966084
  1212.3 106.5 %copy-start.5 = (bf16[2,320,256]{2,1,0:T(8,128)(2,1)S(1)}, bf16[2,320,256]{2,1,0:T(8,128)(2,1)}, u32[]{:S(2)}) copy-start(bf16[2,320,256]{2,1,0:T(8,128)(2,1)} %all-reduce.43.cloned.1.call-done) | copy-start | bytes 983044
  1212.3 106.5 %copy-start.6 = (bf16[1,320,256]{2,1,0:T(8,128)(2,1)S(1)}, bf16[1,320,256]{2,1,0:T(8,128)(2,1)}, u32[]{:S(2)}) copy-start(bf16[1,320,256]{2,1,0:T(8,128)(2,1)} %all-reduce.39.cloned.1.call-done) | copy-start | bytes 491524
  1318.8 5.3 copy-start.1
Sparse Core Ops, SparseCore 0:
  16.6 95.3 all-reduce.20
  139.3 60.0 all-reduce.22
  207.6 64.2 all-reduce.24
  300.6 40.1 all-reduce.26
  346.5 57.1 all-reduce.28
  434.4 35.4 all-reduce.30
  473.0 54.8 all-reduce.32
  568.6 33.9 all-reduce.34
  605.7 53.5 all-reduce.36
  661.6 34.0 all-reduce.38
  705.2 54.7 all-reduce.40
  762.7 35.5 all-reduce.42
  810.0 57.4 all-reduce.44
  871.1 39.7 all-reduce.46
  940.7 64.1 all-reduce.48
  1010.8 59.5 all-reduce.50
  1110.3 92.2 all-reduce.52
  1212.4 104.1 all-reduce.54
where the time goes:
time: 1340 us; the launch traced here: 1330 us
  waiting for transfers between devices  908 us (68%)
  local copies, waits for them, and re-layouts  227 us (17%)
  matrix products  162 us (12%)
  other arithmetic  17.3 us (1%)
  between operations  14.3 us (1%)
    psum x4, waiting for transfers between devices, solve(): lax.psum(partial_value.astype(jnp.bfloat16), 'leaf').astype(jnp.float32)  264 us
    psum x5, waiting for transfers between devices, solve(): lax.psum(division_count.astype(jnp.bfloat16), 'col').astype(jnp.float32)  257 us
    psum x5, waiting for transfers between devices, solve(): lax.psum(division_count.astype(jnp.bfloat16), 'leaf').astype(jnp.float32)  217 us
    psum x4, waiting for transfers between devices, solve(): lax.psum(partial_value.astype(jnp.bfloat16), 'col').astype(jnp.float32)  169 us
    another operation x4, local copies, waits for them, and re-layouts, pair_ancestors(): jnp.stack([climbed[distance][source_node] for source_node, distance in zi...  82.3 us
    dot_general x4, matrix products, solve(): jnp.einsum('boj,boh->bjh', panel_local[initial_position:initial_position...  40.4 us
    dot_general x4, matrix products, forward_products(): jnp.einsum('sjv,svk->sjk', panel_local[chosen], forward_stack[feeders], p...  39.1 us
    gather x4, local copies, waits for them, and re-layouts, forward_products(): panel_local[chosen]  37.9 us
  transfers between devices with their start and end apart: 18, of which 18 were waited for; matrix products, arithmetic and copies ran while one was open for 10% of the time, Pallas kernels for 0%

commit v1 on v0

--- a/solution.py
+++ b/solution.py
@@ -1,8 +1,17 @@
+import functools
+
 import jax
 import jax.numpy as jnp
 import numpy as np
 from jax import lax
+from jax.experimental import pallas as pl
+from jax.experimental.pallas import tpu as pltpu
 from jax.sharding import PartitionSpec as P
+
+MESH = pl.DeviceIdType.MESH
+VMEM_BYTES = 58 * 2**20
+LAG = 2
+
 
 level_starts = (0, 16, 24, 28, 30)
 level_counts = (16, 8, 4, 2, 1)
@@ -132,14 +141,530 @@
     return jnp.concatenate(results, axis=0)
 
 
-def shards(right_side, reciprocal_pivot_matrix, panels, parent):
+def bf16(value):
+    return value.astype(jnp.bfloat16)
+
+
+def f32(value):
+    return value.astype(jnp.float32)
+
+
+def send(src, dst, sems, at, device):
+    return pltpu.make_async_remote_copy(
+        src_ref=src,
+        dst_ref=dst,
+        send_sem=sems[0].at[at],
+        recv_sem=sems[1].at[at],
+        device_id=device,
+        device_id_type=MESH,
+    )
+
+
+class Leaf:
+    def __init__(self, part, result, finish, half_in, first, first_in, second, second_in, sems):
+        self.part, self.result, self.finish = part, result, finish
+        self.half_in, self.first, self.first_in = half_in, first, first_in
+        self.second, self.second_in, self.sems = second, second_in, sems
+        me = lax.axis_index("leaf")
+        self.core = me % 2
+        self.sibling = {"leaf": me + 1 - 2 * self.core}
+        self.along_x = {"leaf": me + 2 - 4 * ((me // 2) % 2)}
+        self.along_y = {"leaf": me + 4 - 8 * (me // 4)}
+        self.half = part.shape[1] // 2
+        self.quarter = self.half // 2
+        self.mine = pl.ds(self.core * self.half, self.half)
+        self.other = pl.ds((1 - self.core) * self.half, self.half)
+
+    def neighbours(self):
+        return (self.sibling, self.along_x, self.along_y)
+
+    def scatter(self, k):
+        return send(self.part.at[k, self.other], self.half_in.at[k], self.sems[0], k, self.sibling)
+
+    def exchange(self, k, step):
+        source, target = ((self.first, self.first_in), (self.second, self.second_in))[step]
+        low, high = pl.ds(0, self.quarter), pl.ds(self.quarter, self.quarter)
+        ways = (self.along_x, self.along_y) if step == 0 else (self.along_y, self.along_x)
+        return (
+            send(source.at[k, low], target.at[k, low], self.sems[1 + 2 * step], k, ways[0]),
+            send(source.at[k, high], target.at[k, high], self.sems[2 + 2 * step], k, ways[1]),
+        )
+
+    def gather(self, k):
+        return send(self.result.at[k, self.mine], self.result.at[k, self.mine], self.sems[5], k, self.sibling)
+
+    def stage_first(self, k):
+        self.scatter(k).wait_recv()
+        self.first[k] = bf16(f32(self.part[k, self.mine]) + f32(self.half_in[k]))
+        for copy in self.exchange(k, 0):
+            copy.start()
+
+    def stage_second(self, k):
+        for copy in self.exchange(k, 0):
+            copy.wait_recv()
+        self.second[k] = bf16(f32(self.first[k]) + f32(self.first_in[k]))
+        for copy in self.exchange(k, 1):
+            copy.start()
+
+    def stage_result(self, k):
+        for copy in self.exchange(k, 1):
+            copy.wait_recv()
+        total = f32(self.second[k]) + f32(self.second_in[k])
+        self.result[k, self.mine] = self.finish(k, self.mine, total)
+        self.gather(k).start()
+
+    def stage_gathered(self, k):
+        self.gather(k).wait_recv()
+
+    def drain(self, k):
+        self.scatter(k).wait_send()
+        for copy in self.exchange(k, 0) + self.exchange(k, 1):
+            copy.wait_send()
+        self.gather(k).wait_send()
+
+
+class Col:
+    def __init__(self, part, result, arrived, joined, joined_in, sems):
+        self.part, self.result, self.arrived = part, result, arrived
+        self.joined, self.joined_in, self.sems = joined, joined_in, sems
+        me = lax.axis_index("col")
+        self.inner = jnp.logical_or(me == 1, me == 2)
+        self.end = jnp.logical_or(me == 0, me == 3)
+        self.end_partner = {"col": (me // 2) + 1}
+        self.inner_partner = {"col": 3 - me}
+        self.outer = {"col": (me // 2) * 3}
+
+    def greet(self, barrier):
+        @pl.when(self.end)
+        def _():
+            pl.semaphore_signal(barrier, inc=1, device_id=self.end_partner, device_id_type=MESH)
+
+        @pl.when(self.inner)
+        def _():
+            pl.semaphore_signal(barrier, inc=1, device_id=self.inner_partner, device_id_type=MESH)
+            pl.semaphore_signal(barrier, inc=1, device_id=self.outer, device_id_type=MESH)
+
+    def to_inner(self, k):
+        return send(self.part.at[k], self.arrived.at[k], self.sems[0], k, self.end_partner)
+
+    def across(self, k):
+        return send(self.joined.at[k], self.joined_in.at[k], self.sems[1], k, self.inner_partner)
+
+    def to_end(self, k):
+        return send(self.result.at[k], self.result.at[k], self.sems[2], k, self.outer)
+
+    def stage_start(self, k):
+        @pl.when(self.end)
+        def _():
+            self.to_inner(k).start()
+
+    def stage_join(self, k):
+        @pl.when(self.inner)
+        def _():
+            self.to_inner(k).wait_recv()
+            self.joined[k] = bf16(f32(self.part[k]) + f32(self.arrived[k]))
+            self.across(k).start()
+
+    def stage_sum(self, k):
+        @pl.when(self.inner)
+        def _():
+            self.across(k).wait_recv()
+            self.result[k] = bf16(f32(self.joined[k]) + f32(self.joined_in[k]))
+            self.to_end(k).start()
+
+    def stage_end(self, k):
+        @pl.when(self.end)
+        def _():
+            self.to_end(k).wait_recv()
+
+    def drain(self, k):
+        @pl.when(self.end)
+        def _():
+            self.to_inner(k).wait_send()
+
+        @pl.when(self.inner)
+        def _():
+            self.across(k).wait_send()
+            self.to_end(k).wait_send()
+
+
+def enter(leaf, col):
+    barrier = pltpu.get_barrier_semaphore()
+    count = 0
+    if leaf is not None:
+        for neighbour in leaf.neighbours():
+            pl.semaphore_signal(barrier, inc=1, device_id=neighbour, device_id_type=MESH)
+        count = 3
+    if col is None:
+        pl.semaphore_wait(barrier, count)
+    else:
+        col.greet(barrier)
+
+        @pl.when(col.end)
+        def _():
+            pl.semaphore_wait(barrier, count + 1)
+
+        @pl.when(col.inner)
+        def _():
+            pl.semaphore_wait(barrier, count + 2)
+
+
+def staged(count, stages):
+    last = max(lag for lag, _ in stages)
+
+    def body(step, carry):
+        for lag, stage in reversed(stages):
+            node = step - lag
+
+            @pl.when(jnp.logical_and(node >= 0, node < count))
+            def _(stage=stage, node=node):
+                stage(node)
+
+        return carry
+
+    lax.fori_loop(0, count + last, body, 0)
+
+
+def each(count, stage):
+    def body(k, carry):
+        stage(k)
+        return carry
+
+    lax.fori_loop(0, count, body, 0)
+
+
+def pair_sems(refs, count):
+    return [(refs[2 * at], refs[2 * at + 1]) for at in range(count)]
+
+
+def forward_kernel(start, count, has_update, *refs):
+    refs = list(refs)
+    take = lambda number: [refs.pop(0) for _ in range(number)]
+    update = take(1)[0] if has_update else None
+    right_hbm, diag_hbm, y_ref, right, diag, load_sem = take(6)
+    part, half_in, first, first_in, second, second_in = take(6)
+    leaf_sems = pair_sems(take(12), 6)
+    leaf = Leaf(
+        part, y_ref, lambda k, rows, total: bf16(total), half_in, first, first_in, second, second_in, leaf_sems
+    )
+    col = None
+    if has_update:
+        summed, arrived, joined, joined_in = take(4)
+        col = Col(update, summed, arrived, joined, joined_in, pair_sems(take(6), 3))
+    loads = [
+        pltpu.make_async_copy(right_hbm.at[pl.ds(start, count)], right, load_sem.at[0]),
+        pltpu.make_async_copy(diag_hbm.at[pl.ds(start, count)], diag, load_sem.at[1]),
+    ]
+    for load in loads:
+        load.start()
+    enter(leaf, col)
+    if has_update:
+        each(count, col.stage_start)
+    for load in loads:
+        load.wait()
+
+    def divide(k):
+        reduced = right[k]
+        if has_update:
+            col.stage_end(k)
+            reduced = reduced - f32(summed[k])
+        part[k] = bf16(jnp.dot(diag[k], bf16(reduced), preferred_element_type=jnp.float32))
+        leaf.scatter(k).start()
+
+    stages = []
+    lag = 0
+    if has_update:
+        stages += [(0, col.stage_join), (LAG, col.stage_sum)]
+        lag = LAG + 1
+    stages += [
+        (lag, divide),
+        (lag + 1, leaf.stage_first),
+        (lag + 1 + LAG, leaf.stage_second),
+        (lag + 1 + 2 * LAG, leaf.stage_result),
+    ]
+    staged(count, stages)
+    each(count, leaf.stage_gathered)
+    each(count, leaf.drain)
+    if has_update:
+        each(count, col.drain)
+
+
+def backward_kernel(start, count, has_update, *refs):
+    refs = list(refs)
+    take = lambda number: [refs.pop(0) for _ in range(number)]
+    update = take(1)[0] if has_update else None
+    y_ref, diag_hbm, x_ref, diag, load_sem, part, arrived, joined, joined_in = take(9)
+    col = Col(part, x_ref, arrived, joined, joined_in, pair_sems(take(6), 3))
+    leaf = None
+    if has_update:
+        z_ref, half_in, first, first_in, second, second_in = take(6)
+
+        def finish(k, rows, total):
+            return bf16(f32(y_ref[k, rows]) - total)
+
+        leaf = Leaf(
+            update, z_ref, finish, half_in, first, first_in, second, second_in, pair_sems(take(12), 6)
+        )
+    load = pltpu.make_async_copy(diag_hbm.at[pl.ds(start, count)], diag, load_sem.at[0])
+    load.start()
+    enter(leaf, col)
+    if has_update:
+        each(count, lambda k: leaf.scatter(k).start())
+    load.wait()
+
+    def divide(k):
+        if has_update:
+            leaf.stage_gathered(k)
+            corrected = z_ref[k]
+        else:
+            corrected = y_ref[k]
+        part[k] = bf16(
+            lax.dot_general(
+                diag[k], corrected, (((0,), (0,)), ((), ())), preferred_element_type=jnp.float32
+            )
+        )
+        col.stage_start(k)
+
+    stages = []
+    lag = 0
+    if has_update:
+        stages += [
+            (0, leaf.stage_first),
+            (LAG, leaf.stage_second),
+            (2 * LAG, leaf.stage_result),
+        ]
+        lag = 2 * LAG + 1
+    stages += [(lag, divide), (lag + LAG, col.stage_join), (lag + 2 * LAG, col.stage_sum)]
+    staged(count, stages)
+    each(count, col.stage_end)
+    each(count, col.drain)
+    if has_update:
+        each(count, leaf.drain)
+
+
+def leaf_scratch(count, rows, rhs):
+    half = pltpu.VMEM((count, rows // 2, rhs), jnp.bfloat16)
+    return [half] * 5
+
+
+def sem_scratch(count, number):
+    return [pltpu.SemaphoreType.DMA((count,))] * (2 * number)
+
+
+def cost(flops, moved):
+    return pl.CostEstimate(flops=flops, bytes_accessed=moved, transcendentals=0)
+
+
+def forward_level(level, update, right_side, diag):
+    start, count = level_starts[level], level_counts[level]
+    rows, depth = diag.shape[1], diag.shape[2]
+    rhs = right_side.shape[2]
+    has_update = update is not None
+    block = pltpu.VMEM((count, depth, rhs), jnp.bfloat16)
+    scratch = [
+        pltpu.VMEM((count, depth, rhs), jnp.float32),
+        pltpu.VMEM((count, rows, depth), jnp.bfloat16),
+        pltpu.SemaphoreType.DMA((2,)),
+        pltpu.VMEM((count, rows, rhs), jnp.bfloat16),
+    ]
+    scratch += leaf_scratch(count, rows, rhs) + sem_scratch(count, 6)
+    if has_update:
+        scratch += [block] * 4 + sem_scratch(count, 3)
+    vmem = pl.BlockSpec(memory_space=pltpu.VMEM)
+    anywhere = pl.BlockSpec(memory_space=pl.ANY)
+    return pl.pallas_call(
+        functools.partial(forward_kernel, start, count, has_update),
+        out_shape=jax.ShapeDtypeStruct((count, rows, rhs), jnp.bfloat16),
+        in_specs=[vmem] * has_update + [anywhere] * 2,
+        out_specs=vmem,
+        scratch_shapes=scratch,
+        name=f"forward_level_{level}",
+        cost_estimate=cost(2 * count * rows * depth * rhs, 2 * count * rows * (depth + rhs)),
+        compiler_params=pltpu.CompilerParams(
+            collective_id=level, has_side_effects=True, vmem_limit_bytes=VMEM_BYTES
+        ),
+    )(*([update] * has_update), right_side, diag)
+
+
+def backward_level(level, update, forward_value, diag):
+    start, count = level_starts[level], level_counts[level]
+    rows, depth = diag.shape[1], diag.shape[2]
+    rhs = forward_value.shape[2]
+    has_update = update is not None
+    block = pltpu.VMEM((count, depth, rhs), jnp.bfloat16)
+    scratch = [pltpu.VMEM((count, rows, depth), jnp.bfloat16), pltpu.SemaphoreType.DMA((1,))]
+    scratch += [block] * 4 + sem_scratch(count, 3)
+    if has_update:
+        scratch += [pltpu.VMEM((count, rows, rhs), jnp.bfloat16)]
+        scratch += leaf_scratch(count, rows, rhs) + sem_scratch(count, 6)
+    vmem = pl.BlockSpec(memory_space=pltpu.VMEM)
+    anywhere = pl.BlockSpec(memory_space=pl.ANY)
+    return pl.pallas_call(
+        functools.partial(backward_kernel, start, count, has_update),
+        out_shape=jax.ShapeDtypeStruct((count, depth, rhs), jnp.bfloat16),
+        in_specs=[vmem] * has_update + [vmem, anywhere],
+        out_specs=vmem,
+        scratch_shapes=scratch,
+        name=f"backward_level_{level}",
+        cost_estimate=cost(2 * count * rows * depth * rhs, 2 * count * rows * (depth + rhs)),
+        compiler_params=pltpu.CompilerParams(
+            collective_id=5 + level, has_side_effects=True, vmem_limit_bytes=VMEM_BYTES
+        ),
+    )(*([update] * has_update), forward_value, diag)
+
+
+def forward_update(level, panels, values, order, feeders):
+    count = level_counts[level]
+    rows, depth = panels.shape[1], panels.shape[2]
+    rhs = values[0].shape[2]
+    lows = [sum(2 ** (level - lower) for lower in range(q)) for q in range(level + 1)]
+    per_node = lows[level]
+    base = sum(
+        level_counts[upper] * sum(2 ** (upper - lower) for lower in range(upper))
+        for upper in range(1, level)
+    )
+
+    def body(order_ref, feeders_ref, panel, *refs):
+        sources, out, total = refs[:level], refs[level], refs[level + 1]
+        m = pl.program_id(1)
+
+        @pl.when(m == 0)
+        def _():
+            total[...] = jnp.zeros_like(total)
+
+        for q in range(level):
+
+            @pl.when(jnp.logical_and(m >= lows[q], m < lows[q + 1]))
+            def _(q=q):
+                total[...] += jnp.dot(panel[0], sources[q][0], preferred_element_type=jnp.float32)
+
+        @pl.when(m == per_node - 1)
+        def _():
+            out[0] = bf16(total[...])
+
+    def panel_at(k, m, order_ref, feeders_ref):
+        return (order_ref[base + k * per_node + m], 0, 0)
+
+    def source_at(q):
+        def at(k, m, order_ref, feeders_ref):
+            near = jnp.minimum(jnp.maximum(m, lows[q]), lows[q + 1] - 1)
+            return (feeders_ref[base + k * per_node + near] - level_starts[q], 0, 0)
+
+        return at
+
+    return pl.pallas_call(
+        body,
+        grid_spec=pltpu.PrefetchScalarGridSpec(
+            num_scalar_prefetch=2,
+            grid=(count, per_node),
+            in_specs=[pl.BlockSpec((1, rows, depth), panel_at)]
+            + [pl.BlockSpec((1, depth, rhs), source_at(q)) for q in range(level)],
+            out_specs=pl.BlockSpec((1, rows, rhs), lambda k, m, *_: (k, 0, 0)),
+            scratch_shapes=[pltpu.VMEM((rows, rhs), jnp.float32)],
+        ),
+        out_shape=jax.ShapeDtypeStruct((count, rows, rhs), jnp.bfloat16),
+        name=f"forward_update_{level}",
+        cost_estimate=cost(
+            2 * count * per_node * rows * depth * rhs, 2 * count * per_node * depth * (rows + rhs)
+        ),
+        compiler_params=pltpu.CompilerParams(vmem_limit_bytes=VMEM_BYTES),
+    )(order, feeders, panels, *values[:level])
+
+
+def backward_update(level, panels, solutions, ancestor):
+    count = level_counts[level]
+    rows, depth = panels.shape[1], panels.shape[2]
+    rhs = solutions[4].shape[2]
+    distances = 4 - level
+    base = pair_offset(level)
+
+    def body(ancestor_ref, *refs):
+        total = None
+        for d in range(distances):
+            product = lax.dot_general(
+                refs[d][0],
+                refs[distances + d][0],
+                (((0,), (0,)), ((), ())),
+                preferred_element_type=jnp.float32,
+            )
+            total = product if total is None else total + product
+        refs[2 * distances][0] = bf16(total)
+
+    def panel_at(d):
+        return lambda k, ancestor_ref: (base + k * distances + d, 0, 0)
+
+    def upper_at(d):
+        above = level + 1 + d
+        return lambda k, ancestor_ref: (
+            ancestor_ref[base + k * distances + d] - level_starts[above],
+            0,
+            0,
+        )
+
+    return pl.pallas_call(
+        body,
+        grid_spec=pltpu.PrefetchScalarGridSpec(
+            num_scalar_prefetch=1,
+            grid=(count,),
+            in_specs=[pl.BlockSpec((1, rows, depth), panel_at(d)) for d in range(distances)]
+            + [pl.BlockSpec((1, rows, rhs), upper_at(d)) for d in range(distances)],
+            out_specs=pl.BlockSpec((1, depth, rhs), lambda k, _: (k, 0, 0)),
+        ),
+        out_shape=jax.ShapeDtypeStruct((count, depth, rhs), jnp.bfloat16),
+        name=f"backward_update_{level}",
+        cost_estimate=cost(
+            2 * count * distances * rows * depth * rhs, 2 * count * distances * rows * (depth + rhs)
+        ),
+        compiler_params=pltpu.CompilerParams(vmem_limit_bytes=VMEM_BYTES),
+    )(ancestor, *([panels] * distances), *[solutions[level + 1 + d] for d in range(distances)])
+
+
+def pairs_by_ancestor(parent):
+    nodes = jnp.arange(parent.shape[0], dtype=jnp.int32)
+    climbed = [parent]
+    for _ in range(3):
+        hit = climbed[-1][:, None] == nodes[None, :]
+        climbed.append(jnp.sum(jnp.where(hit, parent[None, :], 0), axis=1))
+    above = jnp.stack(climbed, axis=1)
+    ancestor = jnp.concatenate(
+        [
+            above[level_starts[q] : level_starts[q] + level_counts[q], : 4 - q].reshape(-1)
+            for q in range(4)
+        ]
+    )
+    sources = jnp.asarray(np.array(pair_table()[0], dtype=np.int32))
+    total = sources.shape[0]
+    here = jnp.arange(total, dtype=jnp.int32)
+    key = ancestor * total + here
+    place = jnp.sum((key[None, :] < key[:, None]).astype(jnp.int32), axis=1)
+    hit = place[None, :] == here[:, None]
+    order = jnp.sum(jnp.where(hit, here[None, :], 0), axis=1)
+    feeders = jnp.sum(jnp.where(hit, sources[None, :], 0), axis=1)
+    return ancestor, order, feeders
+
+
+def shards(right_side, diag, panels, parent):
+    ancestor, order, feeders = pairs_by_ancestor(parent)
+    values = []
+    for level in range(5):
+        update = forward_update(level, panels, values, order, feeders) if level else None
+        values.append(forward_level(level, update, right_side, diag))
+    solutions = [None] * 5
+    for level in (4, 3, 2, 1, 0):
+        update = backward_update(level, panels, solutions, ancestor) if level < 4 else None
+        solutions[level] = backward_level(level, update, values[level], diag)
+    return jnp.concatenate([f32(value) for value in solutions], axis=0)
+
+
+def shards_any(right_side, reciprocal_pivot_matrix, panels, parent):
     ancestor = pair_ancestors(parent)
     return solve(right_side, reciprocal_pivot_matrix, panels, ancestor)
 
 
 def solution(mesh):
+    kernels = mesh.shape["leaf"] == 8 and mesh.shape["col"] == 4
     return jax.shard_map(
-        shards,
+        shards if kernels else shards_any,
         mesh=mesh,
         in_specs=(P(None, "leaf", None), P(None, "col", "leaf"), P(None, "leaf", "col"), P()),
         out_specs=P(None, "leaf", None),

time: 1340 us -> 638 us (0.48)
  waiting for transfers between devices: 908 us -> 0 us
  Pallas kernels: 0 us -> 598 us
  local copies, waits for them, and re-layouts: 227 us -> 23.6 us
  matrix products: 162 us -> 0 us
  between operations: 14.3 us -> 0.16 us
    psum x18 -> x0, waiting for transfers between devices: 908 us -> none  [the longest x4 264 us: solve(): lax.psum(partial_value.astype(jnp.bfloat16), 'leaf').astype(jnp.float32)]
    pallas_call x0 -> x18, Pallas kernels: none -> 598 us  [the longest x5 245 us: backward_level(): pl.pallas_call(functools.partial(backward_kernel, start, count, has_updat...]
    dot_general x22 -> x0, matrix products: 162 us -> none  [the longest x4 40.4 us: solve(): jnp.einsum('boj,boh->bjh', panel_local[initial_position:initial_position...]
    gather x20 -> x0, local copies, waits for them, and re-layouts: 100 us -> none  [the longest x4 37.9 us: forward_products(): panel_local[chosen]]
    another operation x8 -> x0, local copies, waits for them, and re-layouts: 82.3 us -> none  [the longest x4 82.3 us: pair_ancestors(): jnp.stack([climbed[distance][source_node] for source_node, distance in zi...]
    scatter x8 -> x0, local copies, waits for them, and re-layouts: 25.2 us -> none  [the longest x4 15.3 us: solve(): forward_stack.at[start_node:start_node + node_count]]
    unnamed x26 -> x13, local copies, waits for them, and re-layouts: 2.12 us -> 22.2 us
  transfers between devices with their start and end apart: 18 -> 0, of which waited for: 18 -> 0; matrix products, arithmetic and copies ran while one was open for 10% -> 0% of each run, Pallas kernels for 0% -> 0%
where the time goes in v1:
time: 638 us; the launch traced here: 634 us
  Pallas kernels  598 us (94%)
  local copies, waits for them, and re-layouts  23.6 us (4%)
  other arithmetic  11.9 us (2%)
    pallas_call x5, Pallas kernels, backward_level(): pl.pallas_call(functools.partial(backward_kernel, start, count, has_updat...  245 us
    pallas_call x5, Pallas kernels, forward_level(): pl.pallas_call(functools.partial(forward_kernel, start, count, has_update...  229 us
    pallas_call x4, Pallas kernels, forward_update(): pl.pallas_call(body, grid_spec=pltpu.PrefetchScalarGridSpec(num_scalar_pr...  81.8 us
    pallas_call x4, Pallas kernels, backward_update(): pl.pallas_call(body, grid_spec=pltpu.PrefetchScalarGridSpec(num_scalar_pr...  43.2 us
    unnamed x13, local copies, waits for them, and re-layouts  22.2 us

profile of v1, /device:TPU:0, one launch (start us, length us, event | category | flops | bytes accessed | tf_op | source)
XLA Modules:
  0.0 634.2 jit_solution(3991157924107508169)
XLA Ops:
  0.0 0.9 select_reduce_fusion.4
  0.9 0.8 select_reduce_fusion.3
  1.7 0.8 select_reduce_fusion.2
  2.6 0.7 slice.18
  3.3 0.7 pad_add_fusion.2
  4.0 0.1 slice.17
  4.1 0.1 copy.34
  4.2 0.1 reshape.92
  4.2 0.7 pad_add_fusion
  4.9 0.7 pad_add_fusion.1
  5.6 0.1 slice.16
  5.6 0.1 copy.33
  5.7 0.1 reshape.91
  5.8 0.1 copy.32
  5.9 0.1 reshape.90
  6.0 0.6 iota_add_fusion
  6.6 0.2 convert_reduce_fusion
  6.8 1.3 select_reduce_fusion
  8.1 19.9 %copy.35.refs_1_.refs_2_ = bf16[31,640,320]{2,1,0:T(8,128)(2,1)} copy(bf16[31,640,320]{1,2,0:T(8,128)(2,1)} %param.6) | data formatting | bytes 25395200 | tf_op args[1]
  28.0 72.4 %forward_level_0.1.refs_0_.refs_1_ = bf16[16,640,256]{2,1,0:T(8,128)(2,1)} custom-call(f32[31,320,256]{2,1,0:T(8,128)} %refs_1_.12, bf16[31,640,320]{2,1,0:T(8,128)(2,1)} %copy.35.refs_1_.refs_2_), custom_call_target="tpu_custom_call" | custom-call | flops 1677721600 | bytes 11796480 | tf_op jit(solution)/shard_map/forward_level_0/pallas_call | solution.py:475
  100.3 14.0 %forward_update_1.1.refs_0_ = bf16[8,320,256]{2,1,0:T(8,128)(2,1)} custom-call(s32[98]{0:T(128)} %get-tuple-element.6.order_ref, s32[98]{0:T(128)} %get-tuple-element.5.feeders_ref, bf16[98,320,640]{2,1,0:T(8,128)(2,1)} %refs_3_.1, bf16[16,640,256]{2,1,0:T(8,128)(2,1)} %forward_level_0.1.refs_0_.refs_1_), custom_call_target="tpu_custom_call" | custom-call | flops 1677721600 | bytes 11796480 | tf_op jit(solution)/shard_map/forward_update_1/pallas_call | solution.py:555
  114.3 57.8 %forward_level_1.1.refs_1_ = bf16[8,640,256]{2,1,0:T(8,128)(2,1)} custom-call(bf16[8,320,256]{2,1,0:T(8,128)(2,1)} %forward_update_1.1.refs_0_, f32[31,320,256]{2,1,0:T(8,128)} %refs_1_.12, bf16[31,640,320]{2,1,0:T(8,128)(2,1)} %copy.35.refs_1_.refs_2_), custom_call_target="tpu_custom_call" | custom-call | flops 838860800 | bytes 5898240 | tf_op jit(solution)/shard_map/forward_level_1/pallas_call | solution.py:475
  172.1 20.0 %forward_update_2.1.refs_0_ = bf16[4,320,256]{2,1,0:T(8,128)(2,1)} custom-call(s32[98]{0:T(128)} %get-tuple-element.6.order_ref, s32[98]{0:T(128)} %get-tuple-element.5.feeders_ref, bf16[98,320,640]{2,1,0:T(8,128)(2,1)} %refs_3_.1, bf16[16,640,256]{2,1,0:T(8,128)(2,1)} %forward_level_0.1.refs_0_.refs_1_, bf16[8,640,256]{2,1,0:T(8,128)(2,1)} %forward_level_1.1.refs_1_), custom_call_target="tpu_custom_call" | custom-call | flops 2516582400 | bytes 17694720 | tf_op jit(solution)/shard_map/forward_update_2/pallas_call | solution.py:555
  192.1 41.0 %forward_level_2.1.refs_2_.refs_1_ = bf16[4,640,256]{2,1,0:T(8,128)(2,1)} custom-call(bf16[4,320,256]{2,1,0:T(8,128)(2,1)} %forward_update_2.1.refs_0_, f32[31,320,256]{2,1,0:T(8,128)} %refs_1_.12, bf16[31,640,320]{2,1,0:T(8,128)(2,1)} %copy.35.refs_1_.refs_2_), custom_call_target="tpu_custom_call" | custom-call | flops 419430400 | bytes 2949120 | tf_op jit(solution)/shard_map/forward_level_2/pallas_call | solution.py:475
  233.1 23.2 %forward_update_3.1.refs_0_ = bf16[2,320,256]{2,1,0:T(8,128)(2,1)} custom-call(s32[98]{0:T(128)} %get-tuple-element.6.order_ref, s32[98]{0:T(128)} %get-tuple-element.5.feeders_ref, bf16[98,320,640]{2,1,0:T(8,128)(2,1)} %refs_3_.1, bf16[16,640,256]{2,1,0:T(8,128)(2,1)} %forward_level_0.1.refs_0_.refs_1_, bf16[8,640,256]{2,1,0:T(8,128)(2,1)} %forward_level_1.1.refs_1_, ...), custom_call_target="tpu_custom_call" | custom-call | flops 2936012800 | bytes 20643840 | tf_op jit(solution)/shard_map/forward_update_3/pallas_call | solution.py:555
  256.3 30.9 %forward_level_3.1.refs_3_.refs_1_ = bf16[2,640,256]{2,1,0:T(8,128)(2,1)} custom-call(bf16[2,320,256]{2,1,0:T(8,128)(2,1)} %forward_update_3.1.refs_0_, f32[31,320,256]{2,1,0:T(8,128)} %refs_1_.12, bf16[31,640,320]{2,1,0:T(8,128)(2,1)} %copy.35.refs_1_.refs_2_), custom_call_target="tpu_custom_call" | custom-call | flops 209715200 | bytes 1474560 | tf_op jit(solution)/shard_map/forward_level_3/pallas_call | solution.py:475
  287.2 24.7 %forward_update_4.1.refs_0_ = bf16[1,320,256]{2,1,0:T(8,128)(2,1)} custom-call(s32[98]{0:T(128)} %get-tuple-element.6.order_ref, s32[98]{0:T(128)} %get-tuple-element.5.feeders_ref, bf16[98,320,640]{2,1,0:T(8,128)(2,1)} %refs_3_.1, bf16[16,640,256]{2,1,0:T(8,128)(2,1)} %forward_level_0.1.refs_0_.refs_1_, bf16[8,640,256]{2,1,0:T(8,128)(2,1)} %forward_level_1.1.refs_1_, ...), custom_call_target="tpu_custom_call" | custom-call | flops 3145728000 | bytes 22118400 | tf_op jit(solution)/shard_map/forward_update_4/pallas_call | solution.py:555
  311.9 26.5 %forward_level_4.1.refs_0_ = bf16[1,640,256]{2,1,0:T(8,128)(2,1)} custom-call(bf16[1,320,256]{2,1,0:T(8,128)(2,1)} %forward_update_4.1.refs_0_, f32[31,320,256]{2,1,0:T(8,128)} %refs_1_.12, bf16[31,640,320]{2,1,0:T(8,128)(2,1)} %copy.35.refs_1_.refs_2_), custom_call_target="tpu_custom_call" | custom-call | flops 104857600 | bytes 737280 | tf_op jit(solution)/shard_map/forward_level_4/pallas_call | solution.py:475
  338.4 18.8 %backward_level_4.1.refs_1_.refs_3_.refs_5_.refs_7_ = bf16[1,320,256]{2,1,0:T(8,128)(2,1)} custom-call(bf16[1,640,256]{2,1,0:T(8,128)(2,1)} %forward_level_4.1.refs_0_, bf16[31,640,320]{2,1,0:T(8,128)(2,1)} %copy.35.refs_1_.refs_2_), custom_call_target="tpu_custom_call" | custom-call | flops 104857600 | bytes 737280 | tf_op jit(solution)/shard_map/backward_level_4/pallas_call | solution.py:502
  357.2 3.2 backward_update_3.1.refs_0_
  360.4 33.6 %backward_level_3.1.refs_2_.refs_4_.refs_6_ = bf16[2,320,256]{2,1,0:T(8,128)(2,1)} custom-call(bf16[2,640,256]{2,1,0:T(8,128)(2,1)} %backward_update_3.1.refs_0_, bf16[2,640,256]{2,1,0:T(8,128)(2,1)} %forward_level_3.1.refs_3_.refs_1_, bf16[31,640,320]{2,1,0:T(8,128)(2,1)} %copy.35.refs_1_.refs_2_), custom_call_target="tpu_custom_call" | custom-call | flops 209715200 | bytes 1474560 | tf_op jit(solution)/shard_map/backward_level_3/pallas_call | solution.py:502
  394.0 5.6 backward_update_2.1.refs_0_
  399.6 40.2 %backward_level_2.1.refs_3_.refs_5_ = bf16[4,320,256]{2,1,0:T(8,128)(2,1)} custom-call(bf16[4,640,256]{2,1,0:T(8,128)(2,1)} %backward_update_2.1.refs_0_, bf16[4,640,256]{2,1,0:T(8,128)(2,1)} %forward_level_2.1.refs_2_.refs_1_, bf16[31,640,320]{2,1,0:T(8,128)(2,1)} %copy.35.refs_1_.refs_2_), custom_call_target="tpu_custom_call" | custom-call | flops 419430400 | bytes 2949120 | tf_op jit(solution)/shard_map/backward_level_2/pallas_call | solution.py:502
  439.8 11.2 %backward_update_1.1.refs_0_ = bf16[8,640,256]{2,1,0:T(8,128)(2,1)} custom-call(s32[98]{0:T(128)} %get-tuple-element.8.ancestor_ref, bf16[98,320,640]{2,1,0:T(8,128)(2,1)} %refs_3_.1, bf16[98,320,640]{2,1,0:T(8,128)(2,1)} %refs_3_.1, bf16[98,320,640]{2,1,0:T(8,128)(2,1)} %refs_3_.1, bf16[4,320,256]{2,1,0:T(8,128)(2,1)} %backward_level_2.1.refs_3_.refs_5_, ...), custom_call_target="tpu_custom_call" | custom-call | flops 2516582400 | bytes 13762560 | tf_op jit(solution)/shard_map/backward_update_1/pallas_call | solution.py:604
  451.0 60.7 %backward_level_1.1.refs_4_ = bf16[8,320,256]{2,1,0:T(8,128)(2,1)} custom-call(bf16[8,640,256]{2,1,0:T(8,128)(2,1)} %backward_update_1.1.refs_0_, bf16[8,640,256]{2,1,0:T(8,128)(2,1)} %forward_level_1.1.refs_1_, bf16[31,640,320]{2,1,0:T(8,128)(2,1)} %copy.35.refs_1_.refs_2_), custom_call_target="tpu_custom_call" | custom-call | flops 838860800 | bytes 5898240 | tf_op jit(solution)/shard_map/backward_level_1/pallas_call | solution.py:502
  511.7 23.1 %backward_update_0.1.refs_0_ = bf16[16,640,256]{2,1,0:T(8,128)(2,1)} custom-call(s32[98]{0:T(128)} %get-tuple-element.8.ancestor_ref, bf16[98,320,640]{2,1,0:T(8,128)(2,1)} %refs_3_.1, bf16[98,320,640]{2,1,0:T(8,128)(2,1)} %refs_3_.1, bf16[98,320,640]{2,1,0:T(8,128)(2,1)} %refs_3_.1, bf16[98,320,640]{2,1,0:T(8,128)(2,1)} %refs_3_.1, ...), custom_call_target="tpu_custom_call" | custom-call | flops 6710886400 | bytes 36700160 | tf_op jit(solution)/shard_map/backward_update_0/pallas_call | solution.py:604
  534.8 91.7 %backward_level_0.1 = bf16[16,320,256]{2,1,0:T(8,128)(2,1)} custom-call(bf16[16,640,256]{2,1,0:T(8,128)(2,1)} %backward_update_0.1.refs_0_, bf16[16,640,256]{2,1,0:T(8,128)(2,1)} %forward_level_0.1.refs_0_.refs_1_, bf16[31,640,320]{2,1,0:T(8,128)(2,1)} %copy.35.refs_1_.refs_2_), custom_call_target="tpu_custom_call" | custom-call | flops 1677721600 | bytes 11796480 | tf_op jit(solution)/shard_map/backward_level_0/pallas_call | solution.py:502
  626.5 0.0 copy-start
  626.5 0.0 copy-start.1
  626.6 0.0 copy-start.2
  626.6 0.0 copy-start.3
  626.6 2.1 constant_dynamic-update-slice_fusion.4
  628.6 0.0 copy-done
  628.6 0.1 constant_dynamic-update-slice_fusion.3
  628.7 0.1 copy-done.1
  628.8 0.0 copy-done.2
  628.9 0.0 copy-done.3
  628.9 5.3 concatenate.21
  (3 shorter events, 0.1 us)
Async XLA Ops:
  626.5 2.1 copy-start
  626.5 2.3 copy-start.1
  626.6 2.3 copy-start.2
  626.6 2.4 copy-start.3

commit v2 on v1

--- a/solution.py
+++ b/solution.py
@@ -11,6 +11,7 @@
 MESH = pl.DeviceIdType.MESH
 VMEM_BYTES = 58 * 2**20
 LAG = 2
+SPLIT = 2
 
 
 level_starts = (0, 16, 24, 28, 30)
@@ -351,24 +352,36 @@
     if has_update:
         summed, arrived, joined, joined_in = take(4)
         col = Col(update, summed, arrived, joined, joined_in, pair_sems(take(6), 3))
+    units = count * SPLIT
+    width = right.shape[3]
     loads = [
-        pltpu.make_async_copy(right_hbm.at[pl.ds(start, count)], right, load_sem.at[0]),
-        pltpu.make_async_copy(diag_hbm.at[pl.ds(start, count)], diag, load_sem.at[1]),
+        pltpu.make_async_copy(
+            right_hbm.at[pl.ds(start, count), :, pl.ds(half * width, width)], right.at[half], load_sem.at[half]
+        )
+        for half in range(SPLIT)
     ]
+    loads.append(pltpu.make_async_copy(diag_hbm.at[pl.ds(start, count)], diag, load_sem.at[SPLIT]))
     for load in loads:
         load.start()
     enter(leaf, col)
     if has_update:
-        each(count, col.stage_start)
+        each(units, col.stage_start)
     for load in loads:
         load.wait()
 
     def divide(k):
-        reduced = right[k]
+        reduced = right[k % SPLIT, k // SPLIT]
         if has_update:
             col.stage_end(k)
             reduced = reduced - f32(summed[k])
-        part[k] = bf16(jnp.dot(diag[k], bf16(reduced), preferred_element_type=jnp.float32))
+        part[k] = bf16(
+            lax.dot_general(
+                diag[k // SPLIT],
+                bf16(reduced),
+                (((0,), (0,)), ((), ())),
+                preferred_element_type=jnp.float32,
+            )
+        )
         leaf.scatter(k).start()
 
     stages = []
@@ -382,11 +395,11 @@
         (lag + 1 + LAG, leaf.stage_second),
         (lag + 1 + 2 * LAG, leaf.stage_result),
     ]
-    staged(count, stages)
-    each(count, leaf.stage_gathered)
-    each(count, leaf.drain)
-    if has_update:
-        each(count, col.drain)
+    staged(units, stages)
+    each(units, leaf.stage_gathered)
+    each(units, leaf.drain)
+    if has_update:
+        each(units, col.drain)
 
 
 def backward_kernel(start, count, has_update, *refs):
@@ -405,11 +418,12 @@
         leaf = Leaf(
             update, z_ref, finish, half_in, first, first_in, second, second_in, pair_sems(take(12), 6)
         )
+    units = count * SPLIT
     load = pltpu.make_async_copy(diag_hbm.at[pl.ds(start, count)], diag, load_sem.at[0])
     load.start()
     enter(leaf, col)
     if has_update:
-        each(count, lambda k: leaf.scatter(k).start())
+        each(units, lambda k: leaf.scatter(k).start())
     load.wait()
 
     def divide(k):
@@ -418,11 +432,7 @@
             corrected = z_ref[k]
         else:
             corrected = y_ref[k]
-        part[k] = bf16(
-            lax.dot_general(
-                diag[k], corrected, (((0,), (0,)), ((), ())), preferred_element_type=jnp.float32
-            )
-        )
+        part[k] = bf16(jnp.dot(diag[k // SPLIT], corrected, preferred_element_type=jnp.float32))
         col.stage_start(k)
 
     stages = []
@@ -435,20 +445,20 @@
         ]
         lag = 2 * LAG + 1
     stages += [(lag, divide), (lag + LAG, col.stage_join), (lag + 2 * LAG, col.stage_sum)]
-    staged(count, stages)
-    each(count, col.stage_end)
-    each(count, col.drain)
-    if has_update:
-        each(count, leaf.drain)
-
-
-def leaf_scratch(count, rows, rhs):
-    half = pltpu.VMEM((count, rows // 2, rhs), jnp.bfloat16)
+    staged(units, stages)
+    each(units, col.stage_end)
+    each(units, col.drain)
+    if has_update:
+        each(units, leaf.drain)
+
+
+def leaf_scratch(units, rows, width):
+    half = pltpu.VMEM((units, rows // 2, width), jnp.bfloat16)
     return [half] * 5
 
 
-def sem_scratch(count, number):
-    return [pltpu.SemaphoreType.DMA((count,))] * (2 * number)
+def sem_scratch(units, number):
+    return [pltpu.SemaphoreType.DMA((units,))] * (2 * number)
 
 
 def cost(flops, moved):
@@ -457,24 +467,25 @@
 
 def forward_level(level, update, right_side, diag):
     start, count = level_starts[level], level_counts[level]
-    rows, depth = diag.shape[1], diag.shape[2]
+    depth, rows = diag.shape[1], diag.shape[2]
     rhs = right_side.shape[2]
+    units, width = count * SPLIT, rhs // SPLIT
     has_update = update is not None
-    block = pltpu.VMEM((count, depth, rhs), jnp.bfloat16)
+    block = pltpu.VMEM((units, depth, width), jnp.bfloat16)
     scratch = [
-        pltpu.VMEM((count, depth, rhs), jnp.float32),
-        pltpu.VMEM((count, rows, depth), jnp.bfloat16),
-        pltpu.SemaphoreType.DMA((2,)),
-        pltpu.VMEM((count, rows, rhs), jnp.bfloat16),
+        pltpu.VMEM((SPLIT, count, depth, width), jnp.float32),
+        pltpu.VMEM((count, depth, rows), jnp.bfloat16),
+        pltpu.SemaphoreType.DMA((SPLIT + 1,)),
+        pltpu.VMEM((units, rows, width), jnp.bfloat16),
     ]
-    scratch += leaf_scratch(count, rows, rhs) + sem_scratch(count, 6)
-    if has_update:
-        scratch += [block] * 4 + sem_scratch(count, 3)
+    scratch += leaf_scratch(units, rows, width) + sem_scratch(units, 6)
+    if has_update:
+        scratch += [block] * 4 + sem_scratch(units, 3)
     vmem = pl.BlockSpec(memory_space=pltpu.VMEM)
     anywhere = pl.BlockSpec(memory_space=pl.ANY)
     return pl.pallas_call(
         functools.partial(forward_kernel, start, count, has_update),
-        out_shape=jax.ShapeDtypeStruct((count, rows, rhs), jnp.bfloat16),
+        out_shape=jax.ShapeDtypeStruct((units, rows, width), jnp.bfloat16),
         in_specs=[vmem] * has_update + [anywhere] * 2,
         out_specs=vmem,
         scratch_shapes=scratch,
@@ -488,118 +499,128 @@
 
 def backward_level(level, update, forward_value, diag):
     start, count = level_starts[level], level_counts[level]
-    rows, depth = diag.shape[1], diag.shape[2]
-    rhs = forward_value.shape[2]
+    depth, rows = diag.shape[1], diag.shape[2]
+    units, width = forward_value.shape[0], forward_value.shape[2]
     has_update = update is not None
-    block = pltpu.VMEM((count, depth, rhs), jnp.bfloat16)
-    scratch = [pltpu.VMEM((count, rows, depth), jnp.bfloat16), pltpu.SemaphoreType.DMA((1,))]
-    scratch += [block] * 4 + sem_scratch(count, 3)
-    if has_update:
-        scratch += [pltpu.VMEM((count, rows, rhs), jnp.bfloat16)]
-        scratch += leaf_scratch(count, rows, rhs) + sem_scratch(count, 6)
+    block = pltpu.VMEM((units, depth, width), jnp.bfloat16)
+    scratch = [pltpu.VMEM((count, depth, rows), jnp.bfloat16), pltpu.SemaphoreType.DMA((1,))]
+    scratch += [block] * 4 + sem_scratch(units, 3)
+    if has_update:
+        scratch += [pltpu.VMEM((units, rows, width), jnp.bfloat16)]
+        scratch += leaf_scratch(units, rows, width) + sem_scratch(units, 6)
     vmem = pl.BlockSpec(memory_space=pltpu.VMEM)
     anywhere = pl.BlockSpec(memory_space=pl.ANY)
     return pl.pallas_call(
         functools.partial(backward_kernel, start, count, has_update),
-        out_shape=jax.ShapeDtypeStruct((count, depth, rhs), jnp.bfloat16),
+        out_shape=jax.ShapeDtypeStruct((units, depth, width), jnp.bfloat16),
         in_specs=[vmem] * has_update + [vmem, anywhere],
         out_specs=vmem,
         scratch_shapes=scratch,
         name=f"backward_level_{level}",
-        cost_estimate=cost(2 * count * rows * depth * rhs, 2 * count * rows * (depth + rhs)),
+        cost_estimate=cost(2 * units * rows * depth * width, 2 * count * rows * depth),
         compiler_params=pltpu.CompilerParams(
             collective_id=5 + level, has_side_effects=True, vmem_limit_bytes=VMEM_BYTES
         ),
     )(*([update] * has_update), forward_value, diag)
 
 
-def forward_update(level, panels, values, order, feeders):
-    count = level_counts[level]
+def climb(parent_ref, node, distance):
+    for _ in range(distance):
+        node = parent_ref[node]
+    return node
+
+
+def joined_columns(ref):
+    return jnp.concatenate([ref[half] for half in range(SPLIT)], axis=1)
+
+
+def forward_update(level, panels, value, earlier, parent):
+    count, start = level_counts[level], level_starts[level]
     rows, depth = panels.shape[1], panels.shape[2]
-    rhs = values[0].shape[2]
-    lows = [sum(2 ** (level - lower) for lower in range(q)) for q in range(level + 1)]
-    per_node = lows[level]
-    base = sum(
-        level_counts[upper] * sum(2 ** (upper - lower) for lower in range(upper))
-        for upper in range(1, level)
-    )
-
-    def body(order_ref, feeders_ref, panel, *refs):
-        sources, out, total = refs[:level], refs[level], refs[level + 1]
-        m = pl.program_id(1)
-
-        @pl.when(m == 0)
-        def _():
-            total[...] = jnp.zeros_like(total)
-
-        for q in range(level):
-
-            @pl.when(jnp.logical_and(m >= lows[q], m < lows[q + 1]))
-            def _(q=q):
-                total[...] += jnp.dot(panel[0], sources[q][0], preferred_element_type=jnp.float32)
-
-        @pl.when(m == per_node - 1)
-        def _():
-            out[0] = bf16(total[...])
-
-    def panel_at(k, m, order_ref, feeders_ref):
-        return (order_ref[base + k * per_node + m], 0, 0)
-
-    def source_at(q):
-        def at(k, m, order_ref, feeders_ref):
-            near = jnp.minimum(jnp.maximum(m, lows[q]), lows[q + 1] - 1)
-            return (feeders_ref[base + k * per_node + near] - level_starts[q], 0, 0)
-
-        return at
-
-    return pl.pallas_call(
+    width = value.shape[2]
+    rhs = width * SPLIT
+    distances = 4 - level
+    base = pair_offset(level)
+    above = level_counts[level + 1 :]
+    given = len(earlier)
+
+    def body(parent_ref, *refs):
+        panel, values, before = refs[:distances], refs[distances], refs[distances + 1 : distances + 1 + given]
+        done, beyond, total = refs[distances + 1 + given], refs[distances + 2 + given : -1], refs[-1]
+        sums = (total, *beyond)
+        k = pl.program_id(0)
+
+        @pl.when(k == 0)
+        def _():
+            for at in range(distances):
+                sums[at][...] = before[at][...] if given else jnp.zeros_like(sums[at])
+
+        known = joined_columns(values)
+        node = start + k
+        for at in range(distances):
+            node = parent_ref[node]
+            slot = node - level_starts[level + 1 + at]
+            sums[at][slot] += jnp.dot(panel[at][0], known, preferred_element_type=jnp.float32)
+
+        @pl.when(k == count - 1)
+        def _():
+            for slot in range(above[0]):
+                for half in range(SPLIT):
+                    done[slot * SPLIT + half] = bf16(total[slot, :, half * width : (half + 1) * width])
+
+    def panel_at(d):
+        return lambda k, parent_ref: (base + k * distances + d, 0, 0)
+
+    whole = lambda shape: pl.BlockSpec(shape, lambda k, parent_ref: (0, 0, 0))
+    shapes = [(number, rows, rhs) for number in above]
+    outs = pl.pallas_call(
         body,
         grid_spec=pltpu.PrefetchScalarGridSpec(
-            num_scalar_prefetch=2,
-            grid=(count, per_node),
-            in_specs=[pl.BlockSpec((1, rows, depth), panel_at)]
-            + [pl.BlockSpec((1, depth, rhs), source_at(q)) for q in range(level)],
-            out_specs=pl.BlockSpec((1, rows, rhs), lambda k, m, *_: (k, 0, 0)),
-            scratch_shapes=[pltpu.VMEM((rows, rhs), jnp.float32)],
+            num_scalar_prefetch=1,
+            grid=(count,),
+            in_specs=[pl.BlockSpec((1, rows, depth), panel_at(d)) for d in range(distances)]
+            + [pl.BlockSpec((SPLIT, depth, width), lambda k, parent_ref: (k, 0, 0))]
+            + [whole(shape) for shape in shapes[: given]],
+            out_specs=[whole((above[0] * SPLIT, rows, width))] + [whole(shape) for shape in shapes[1:]],
+            scratch_shapes=[pltpu.VMEM(shapes[0], jnp.float32)],
         ),
-        out_shape=jax.ShapeDtypeStruct((count, rows, rhs), jnp.bfloat16),
+        out_shape=[jax.ShapeDtypeStruct((above[0] * SPLIT, rows, width), jnp.bfloat16)]
+        + [jax.ShapeDtypeStruct(shape, jnp.float32) for shape in shapes[1:]],
         name=f"forward_update_{level}",
         cost_estimate=cost(
-            2 * count * per_node * rows * depth * rhs, 2 * count * per_node * depth * (rows + rhs)
+            2 * count * distances * rows * depth * rhs, 2 * count * depth * (distances * rows + rhs)
         ),
         compiler_params=pltpu.CompilerParams(vmem_limit_bytes=VMEM_BYTES),
-    )(order, feeders, panels, *values[:level])
-
-
-def backward_update(level, panels, solutions, ancestor):
-    count = level_counts[level]
+    )(parent, *([panels] * distances), value, *earlier)
+    return outs[0], outs[1:]
+
+
+def backward_update(level, panels, solutions, parent):
+    count, start = level_counts[level], level_starts[level]
     rows, depth = panels.shape[1], panels.shape[2]
-    rhs = solutions[4].shape[2]
+    width = solutions[4].shape[2]
     distances = 4 - level
     base = pair_offset(level)
 
-    def body(ancestor_ref, *refs):
+    def body(parent_ref, *refs):
         total = None
         for d in range(distances):
             product = lax.dot_general(
                 refs[d][0],
-                refs[distances + d][0],
+                joined_columns(refs[distances + d]),
                 (((0,), (0,)), ((), ())),
                 preferred_element_type=jnp.float32,
             )
             total = product if total is None else total + product
-        refs[2 * distances][0] = bf16(total)
+        for half in range(SPLIT):
+            refs[2 * distances][half] = bf16(total[:, half * width : (half + 1) * width])
 
     def panel_at(d):
-        return lambda k, ancestor_ref: (base + k * distances + d, 0, 0)
+        return lambda k, parent_ref: (base + k * distances + d, 0, 0)
 
     def upper_at(d):
-        above = level + 1 + d
-        return lambda k, ancestor_ref: (
-            ancestor_ref[base + k * distances + d] - level_starts[above],
-            0,
-            0,
-        )
+        first = level_starts[level + 1 + d]
+        return lambda k, parent_ref: (climb(parent_ref, start + k, d + 1) - first, 0, 0)
 
     return pl.pallas_call(
         body,
@@ -607,53 +628,56 @@
             num_scalar_prefetch=1,
             grid=(count,),
             in_specs=[pl.BlockSpec((1, rows, depth), panel_at(d)) for d in range(distances)]
-            + [pl.BlockSpec((1, rows, rhs), upper_at(d)) for d in range(distances)],
-            out_specs=pl.BlockSpec((1, depth, rhs), lambda k, _: (k, 0, 0)),
+            + [pl.BlockSpec((SPLIT, rows, width), upper_at(d)) for d in range(distances)],
+            out_specs=pl.BlockSpec((SPLIT, depth, width), lambda k, _: (k, 0, 0)),
         ),
-        out_shape=jax.ShapeDtypeStruct((count, depth, rhs), jnp.bfloat16),
+        out_shape=jax.ShapeDtypeStruct((count * SPLIT, depth, width), jnp.bfloat16),
         name=f"backward_update_{level}",
         cost_estimate=cost(
-            2 * count * distances * rows * depth * rhs, 2 * count * distances * rows * (depth + rhs)
+            2 * count * distances * rows * depth * width * SPLIT, 2 * count * distances * rows * depth
         ),
         compiler_params=pltpu.CompilerParams(vmem_limit_bytes=VMEM_BYTES),
-    )(ancestor, *([panels] * distances), *[solutions[level + 1 + d] for d in range(distances)])
-
-
-def pairs_by_ancestor(parent):
-    nodes = jnp.arange(parent.shape[0], dtype=jnp.int32)
-    climbed = [parent]
-    for _ in range(3):
-        hit = climbed[-1][:, None] == nodes[None, :]
-        climbed.append(jnp.sum(jnp.where(hit, parent[None, :], 0), axis=1))
-    above = jnp.stack(climbed, axis=1)
-    ancestor = jnp.concatenate(
-        [
-            above[level_starts[q] : level_starts[q] + level_counts[q], : 4 - q].reshape(-1)
-            for q in range(4)
-        ]
-    )
-    sources = jnp.asarray(np.array(pair_table()[0], dtype=np.int32))
-    total = sources.shape[0]
-    here = jnp.arange(total, dtype=jnp.int32)
-    key = ancestor * total + here
-    place = jnp.sum((key[None, :] < key[:, None]).astype(jnp.int32), axis=1)
-    hit = place[None, :] == here[:, None]
-    order = jnp.sum(jnp.where(hit, here[None, :], 0), axis=1)
-    feeders = jnp.sum(jnp.where(hit, sources[None, :], 0), axis=1)
-    return ancestor, order, feeders
-
-
-def shards(right_side, diag, panels, parent):
-    ancestor, order, feeders = pairs_by_ancestor(parent)
-    values = []
-    for level in range(5):
-        update = forward_update(level, panels, values, order, feeders) if level else None
-        values.append(forward_level(level, update, right_side, diag))
+    )(parent, *([panels] * distances), *[solutions[level + 1 + d] for d in range(distances)])
+
+
+def assemble(solutions, node_total):
+    rows, width = solutions[0].shape[1], solutions[0].shape[2]
+
+    def body(*refs):
+        out = refs[5]
+        for level in range(5):
+
+            def store(k, level=level):
+                for half in range(SPLIT):
+                    out[level_starts[level] + k, :, half * width : (half + 1) * width] = f32(
+                        refs[level][k * SPLIT + half]
+                    )
+
+            each(level_counts[level], store)
+
+    return pl.pallas_call(
+        body,
+        out_shape=jax.ShapeDtypeStruct((node_total, rows, width * SPLIT), jnp.float32),
+        in_specs=[pl.BlockSpec(memory_space=pltpu.VMEM)] * 5,
+        out_specs=pl.BlockSpec(memory_space=pltpu.VMEM),
+        name="assemble",
+        cost_estimate=cost(0, node_total * rows * width * SPLIT * 6),
+        compiler_params=pltpu.CompilerParams(vmem_limit_bytes=VMEM_BYTES),
+    )(*solutions)
+
+
+def shards(right_side, reciprocal_pivot_matrix, panels, parent):
+    diag = jnp.swapaxes(reciprocal_pivot_matrix, 1, 2)
+    values = [forward_level(0, None, right_side, diag)]
+    earlier = ()
+    for level in range(4):
+        update, earlier = forward_update(level, panels, values[level], earlier, parent)
+        values.append(forward_level(level + 1, update, right_side, diag))
     solutions = [None] * 5
     for level in (4, 3, 2, 1, 0):
-        update = backward_update(level, panels, solutions, ancestor) if level < 4 else None
+        update = backward_update(level, panels, solutions, parent) if level < 4 else None
         solutions[level] = backward_level(level, update, values[level], diag)
-    return jnp.concatenate([f32(value) for value in solutions], axis=0)
+    return assemble(solutions, right_side.shape[0])
 
 
 def shards_any(right_side, reciprocal_pivot_matrix, panels, parent):

time: 638 us -> 565 us (0.89)
  Pallas kernels: 598 us -> 563 us
  local copies, waits for them, and re-layouts: 23.6 us -> 0 us
  other arithmetic: 11.9 us -> 0 us
    pallas_call x4, Pallas kernels: 81.8 us -> 42.5 us  [forward_update(): pl.pallas_call(body, grid_spec=pltpu.PrefetchScalarGridSpec(num_scalar_pr...]
    unnamed x13 -> x0, local copies, waits for them, and re-layouts: 22.2 us -> none
    pallas_call x0 -> x1, Pallas kernels: none -> 7.13 us  [assemble(): pl.pallas_call(body, out_shape=jax.ShapeDtypeStruct((node_total, rows, wi...]
where the time goes in v2:
time: 565 us; the launch traced here: 563 us
  Pallas kernels  563 us (100%)
    pallas_call x5, Pallas kernels, backward_level(): pl.pallas_call(functools.partial(backward_kernel, start, count, has_updat...  239 us
    pallas_call x5, Pallas kernels, forward_level(): pl.pallas_call(functools.partial(forward_kernel, start, count, has_update...  231 us
    pallas_call x4, Pallas kernels, backward_update(): pl.pallas_call(body, grid_spec=pltpu.PrefetchScalarGridSpec(num_scalar_pr...  42.9 us
    pallas_call x4, Pallas kernels, forward_update(): pl.pallas_call(body, grid_spec=pltpu.PrefetchScalarGridSpec(num_scalar_pr...  42.5 us

profile of v2, /device:TPU:0, one launch (start us, length us, event | category | flops | bytes accessed | tf_op | source)
XLA Modules:
  0.0 562.9 jit_solution(7274804611808274315)
XLA Ops:
  0.0 78.5 %forward_level_0.1.refs_4_.refs_1_ = bf16[32,640,128]{2,1,0:T(8,128)(2,1)} custom-call(f32[31,320,256]{2,1,0:T(8,128)} %refs_1_.16, bf16[31,320,640]{2,1,0:T(8,128)(2,1)} %bitcast.1), custom_call_target="tpu_custom_call" | custom-call | flops 1677721600 | bytes 11796480 | tf_op jit(solution)/shard_map/forward_level_0/pallas_call | solution.py:486
  78.5 21.8 %forward_update_0.1 = (bf16[16,320,128]{2,1,0:T(8,128)(2,1)}, f32[4,320,256]{2,1,0:T(8,128)}, f32[2,320,256]{2,1,0:T(8,128)}, f32[1,320,256]{2,1,0:T(8,128)}) custom-call(s32[31]{0:T(128)} %parent_ref.15, bf16[98,320,640]{2,1,0:T(8,128)(2,1)} %refs_3_.3, bf16[98,320,640]{2,1,0:T(8,128)(2,1)} %refs_3_.3, bf16[98,320,640]{2,1,0:T(8,128)(2,1)} %refs_3_.3, ...), custom_call_target="tpu_custom_call" | custom-call | flops 6710886400 | bytes 31457280 | tf_op jit(solution)/shard_map/forward_update_0/pallas_call | solution.py:576
  100.3 58.3 %forward_level_1.1.refs_3_.refs_1_ = bf16[16,640,128]{2,1,0:T(8,128)(2,1)} custom-call(bf16[16,320,128]{2,1,0:T(8,128)(2,1)} %get-tuple-element.14.refs_0_, f32[31,320,256]{2,1,0:T(8,128)} %refs_1_.16, bf16[31,320,640]{2,1,0:T(8,128)(2,1)} %bitcast.2), custom_call_target="tpu_custom_call" | custom-call | flops 838860800 | bytes 5898240 | tf_op jit(solution)/shard_map/forward_level_1/pallas_call | solution.py:486
  158.6 11.6 %forward_update_1.1 = (bf16[8,320,128]{2,1,0:T(8,128)(2,1)}, f32[2,320,256]{2,1,0:T(8,128)}, f32[1,320,256]{2,1,0:T(8,128)}) custom-call(s32[31]{0:T(128)} %parent_ref.15, bf16[98,320,640]{2,1,0:T(8,128)(2,1)} %refs_3_.3, bf16[98,320,640]{2,1,0:T(8,128)(2,1)} %refs_3_.3, bf16[98,320,640]{2,1,0:T(8,128)(2,1)} %refs_3_.3, ...), custom_call_target="tpu_custom_call" | custom-call | flops 2516582400 | bytes 12451840 | tf_op jit(solution)/shard_map/forward_update_1/pallas_call | solution.py:576
  170.2 39.3 %forward_level_2.1.refs_2_.refs_1_ = bf16[8,640,128]{2,1,0:T(8,128)(2,1)} custom-call(bf16[8,320,128]{2,1,0:T(8,128)(2,1)} %get-tuple-element.18.refs_0_, f32[31,320,256]{2,1,0:T(8,128)} %refs_1_.16, bf16[31,320,640]{2,1,0:T(8,128)(2,1)} %bitcast.3), custom_call_target="tpu_custom_call" | custom-call | flops 419430400 | bytes 2949120 | tf_op jit(solution)/shard_map/forward_level_2/pallas_call | solution.py:486
  209.5 5.9 %forward_update_2.1 = (bf16[4,320,128]{2,1,0:T(8,128)(2,1)}, f32[1,320,256]{2,1,0:T(8,128)}) custom-call(s32[31]{0:T(128)} %parent_ref.15, bf16[98,320,640]{2,1,0:T(8,128)(2,1)} %refs_3_.3, bf16[98,320,640]{2,1,0:T(8,128)(2,1)} %refs_3_.3, bf16[8,640,128]{2,1,0:T(8,128)(2,1)} %forward_level_2.1.refs_2_.refs_1_, f32[2,320,256]{2,1,0:T(8,128)} %get-tuple-element.19.refs_3_, ...), custom_call_target="tpu_custom_call" | custom-call | flops 838860800 | bytes 4587520 | tf_op jit(solution)/shard_map/forward_update_2/pallas_call | solution.py:576
  215.4 29.4 %forward_level_3.1.refs_1_ = bf16[4,640,128]{2,1,0:T(8,128)(2,1)} custom-call(bf16[4,320,128]{2,1,0:T(8,128)(2,1)} %get-tuple-element.21.refs_0_, f32[31,320,256]{2,1,0:T(8,128)} %refs_1_.16, bf16[31,320,640]{2,1,0:T(8,128)(2,1)} %bitcast.4), custom_call_target="tpu_custom_call" | custom-call | flops 209715200 | bytes 1474560 | tf_op jit(solution)/shard_map/forward_level_3/pallas_call | solution.py:486
  244.8 3.2 forward_update_3.1.refs_0_
  248.0 25.7 %forward_level_4.1.refs_0_ = bf16[2,640,128]{2,1,0:T(8,128)(2,1)} custom-call(bf16[2,320,128]{2,1,0:T(8,128)(2,1)} %forward_update_3.1.refs_0_, f32[31,320,256]{2,1,0:T(8,128)} %refs_1_.16, bf16[31,320,640]{2,1,0:T(8,128)(2,1)} %bitcast.5), custom_call_target="tpu_custom_call" | custom-call | flops 104857600 | bytes 737280 | tf_op jit(solution)/shard_map/forward_level_4/pallas_call | solution.py:486
  273.7 16.1 %backward_level_4.1.refs_1_.refs_3_.refs_5_.refs_7_.refs_4_ = bf16[2,320,128]{2,1,0:T(8,128)(2,1)} custom-call(bf16[2,640,128]{2,1,0:T(8,128)(2,1)} %forward_level_4.1.refs_0_, bf16[31,320,640]{2,1,0:T(8,128)(2,1)} %bitcast.6), custom_call_target="tpu_custom_call" | custom-call | flops 104857600 | bytes 409600 | tf_op jit(solution)/shard_map/backward_level_4/pallas_call | solution.py:513
  289.9 3.2 backward_update_3.1.refs_0_
  293.1 28.7 %backward_level_3.1.refs_2_.refs_4_.refs_6_.refs_3_ = bf16[4,320,128]{2,1,0:T(8,128)(2,1)} custom-call(bf16[4,640,128]{2,1,0:T(8,128)(2,1)} %backward_update_3.1.refs_0_, bf16[4,640,128]{2,1,0:T(8,128)(2,1)} %forward_level_3.1.refs_1_, bf16[31,320,640]{2,1,0:T(8,128)(2,1)} %bitcast.7), custom_call_target="tpu_custom_call" | custom-call | flops 209715200 | bytes 819200 | tf_op jit(solution)/shard_map/backward_level_3/pallas_call | solution.py:513
  321.8 5.7 %backward_update_2.1.refs_0_ = bf16[8,640,128]{2,1,0:T(8,128)(2,1)} custom-call(s32[31]{0:T(128)} %parent_ref.15, bf16[98,320,640]{2,1,0:T(8,128)(2,1)} %refs_3_.3, bf16[98,320,640]{2,1,0:T(8,128)(2,1)} %refs_3_.3, bf16[4,320,128]{2,1,0:T(8,128)(2,1)} %backward_level_3.1.refs_2_.refs_4_.refs_6_.refs_3_, ...), custom_call_target="tpu_custom_call" | custom-call | flops 838860800 | bytes 3276800 | tf_op jit(solution)/shard_map/backward_update_2/pallas_call | solution.py:625
  327.5 38.0 %backward_level_2.1.refs_3_.refs_5_.refs_2_ = bf16[8,320,128]{2,1,0:T(8,128)(2,1)} custom-call(bf16[8,640,128]{2,1,0:T(8,128)(2,1)} %backward_update_2.1.refs_0_, bf16[8,640,128]{2,1,0:T(8,128)(2,1)} %forward_level_2.1.refs_2_.refs_1_, bf16[31,320,640]{2,1,0:T(8,128)(2,1)} %bitcast.8), custom_call_target="tpu_custom_call" | custom-call | flops 419430400 | bytes 1638400 | tf_op jit(solution)/shard_map/backward_level_2/pallas_call | solution.py:513
  365.5 11.2 %backward_update_1.1.refs_0_ = bf16[16,640,128]{2,1,0:T(8,128)(2,1)} custom-call(s32[31]{0:T(128)} %parent_ref.15, bf16[98,320,640]{2,1,0:T(8,128)(2,1)} %refs_3_.3, bf16[98,320,640]{2,1,0:T(8,128)(2,1)} %refs_3_.3, bf16[98,320,640]{2,1,0:T(8,128)(2,1)} %refs_3_.3, bf16[8,320,128]{2,1,0:T(8,128)(2,1)} %backward_level_2.1.refs_3_.refs_5_.refs_2_, ...), custom_call_target="tpu_custom_call" | custom-call | flops 2516582400 | bytes 9830400 | tf_op jit(solution)/shard_map/backward_update_1/pallas_call | solution.py:625
  376.7 58.3 %backward_level_1.1.refs_4_.refs_1_ = bf16[16,320,128]{2,1,0:T(8,128)(2,1)} custom-call(bf16[16,640,128]{2,1,0:T(8,128)(2,1)} %backward_update_1.1.refs_0_, bf16[16,640,128]{2,1,0:T(8,128)(2,1)} %forward_level_1.1.refs_3_.refs_1_, bf16[31,320,640]{2,1,0:T(8,128)(2,1)} %bitcast.9), custom_call_target="tpu_custom_call" | custom-call | flops 838860800 | bytes 3276800 | tf_op jit(solution)/shard_map/backward_level_1/pallas_call | solution.py:513
  435.0 22.9 %backward_update_0.1.refs_0_ = bf16[32,640,128]{2,1,0:T(8,128)(2,1)} custom-call(s32[31]{0:T(128)} %parent_ref.15, bf16[98,320,640]{2,1,0:T(8,128)(2,1)} %refs_3_.3, bf16[98,320,640]{2,1,0:T(8,128)(2,1)} %refs_3_.3, bf16[98,320,640]{2,1,0:T(8,128)(2,1)} %refs_3_.3, bf16[98,320,640]{2,1,0:T(8,128)(2,1)} %refs_3_.3, ...), custom_call_target="tpu_custom_call" | custom-call | flops 6710886400 | bytes 26214400 | tf_op jit(solution)/shard_map/backward_update_0/pallas_call | solution.py:625
  457.9 97.9 %backward_level_0.1.refs_0_ = bf16[32,320,128]{2,1,0:T(8,128)(2,1)} custom-call(bf16[32,640,128]{2,1,0:T(8,128)(2,1)} %backward_update_0.1.refs_0_, bf16[32,640,128]{2,1,0:T(8,128)(2,1)} %forward_level_0.1.refs_4_.refs_1_, bf16[31,320,640]{2,1,0:T(8,128)(2,1)} %bitcast.10), custom_call_target="tpu_custom_call" | custom-call | flops 1677721600 | bytes 6553600 | tf_op jit(solution)/shard_map/backward_level_0/pallas_call | solution.py:513
  555.8 7.1 %assemble.1 = f32[31,320,256]{2,1,0:T(8,128)} custom-call(bf16[32,320,128]{2,1,0:T(8,128)(2,1)} %backward_level_0.1.refs_0_, bf16[16,320,128]{2,1,0:T(8,128)(2,1)} %backward_level_1.1.refs_4_.refs_1_, bf16[8,320,128]{2,1,0:T(8,128)(2,1)} %backward_level_2.1.refs_3_.refs_5_.refs_2_, bf16[4,320,128]{2,1,0:T(8,128)(2,1)} %backward_level_3.1.refs_2_.refs_4_.refs_6_.refs_3_, ...), custom_call_target="tpu_custom_call" | custom-call | bytes 15237120 | tf_op jit(solution)/shard_map/assemble/pallas_call | solution.py:658

commit v3 on v2

--- a/solution.py
+++ b/solution.py
@@ -11,7 +11,7 @@
 MESH = pl.DeviceIdType.MESH
 VMEM_BYTES = 58 * 2**20
 LAG = 2
-SPLIT = 2
+SPLITS = (1, 2, 2, 2, 2)
 
 
 level_starts = (0, 16, 24, 28, 30)
@@ -352,15 +352,15 @@
     if has_update:
         summed, arrived, joined, joined_in = take(4)
         col = Col(update, summed, arrived, joined, joined_in, pair_sems(take(6), 3))
-    units = count * SPLIT
-    width = right.shape[3]
+    split, width = right.shape[0], right.shape[3]
+    units = count * split
     loads = [
         pltpu.make_async_copy(
             right_hbm.at[pl.ds(start, count), :, pl.ds(half * width, width)], right.at[half], load_sem.at[half]
         )
-        for half in range(SPLIT)
+        for half in range(split)
     ]
-    loads.append(pltpu.make_async_copy(diag_hbm.at[pl.ds(start, count)], diag, load_sem.at[SPLIT]))
+    loads.append(pltpu.make_async_copy(diag_hbm.at[pl.ds(start, count)], diag, load_sem.at[split]))
     for load in loads:
         load.start()
     enter(leaf, col)
@@ -370,13 +370,13 @@
         load.wait()
 
     def divide(k):
-        reduced = right[k % SPLIT, k // SPLIT]
+        reduced = right[k % split, k // split]
         if has_update:
             col.stage_end(k)
             reduced = reduced - f32(summed[k])
         part[k] = bf16(
             lax.dot_general(
-                diag[k // SPLIT],
+                diag[k // split],
                 bf16(reduced),
                 (((0,), (0,)), ((), ())),
                 preferred_element_type=jnp.float32,
@@ -395,30 +395,73 @@
         (lag + 1 + LAG, leaf.stage_second),
         (lag + 1 + 2 * LAG, leaf.stage_result),
     ]
+
+    def finish(k):
+        leaf.stage_gathered(k)
+        leaf.drain(k)
+        if has_update:
+            col.drain(k)
+
+    stages.append((lag + 1 + 3 * LAG, finish))
     staged(units, stages)
-    each(units, leaf.stage_gathered)
-    each(units, leaf.drain)
-    if has_update:
-        each(units, col.drain)
-
-
-def backward_kernel(start, count, has_update, *refs):
+
+
+def backward_kernel(start, count, units, has_update, lower, uppers, *refs):
     refs = list(refs)
     take = lambda number: [refs.pop(0) for _ in range(number)]
     update = take(1)[0] if has_update else None
-    y_ref, diag_hbm, x_ref, diag, load_sem, part, arrived, joined, joined_in = take(9)
+    y_ref, diag_hbm = take(2)
+    if lower is not None:
+        parent_ref, panels_hbm = take(2)
+        known = take(len(uppers))
+    x_ref = take(1)[0]
+    if lower is not None:
+        partial_ref = take(1)[0]
+    diag, load_sem, part, arrived, joined, joined_in = take(6)
     col = Col(part, x_ref, arrived, joined, joined_in, pair_sems(take(6), 3))
     leaf = None
     if has_update:
         z_ref, half_in, first, first_in, second, second_in = take(6)
 
-        def finish(k, rows, total):
+        def corrected_half(k, rows, total):
             return bf16(f32(y_ref[k, rows]) - total)
 
         leaf = Leaf(
-            update, z_ref, finish, half_in, first, first_in, second, second_in, pair_sems(take(12), 6)
-        )
-    units = count * SPLIT
+            update, z_ref, corrected_half, half_in, first, first_in, second, second_in, pair_sems(take(12), 6)
+        )
+    if lower is not None:
+        panel, panel_sem = take(2)
+        distances = 4 - lower
+
+        def fetch(k):
+            at = pair_offset(lower) + k * distances + 1
+            return pltpu.make_async_copy(
+                panels_hbm.at[pl.ds(at, distances - 1)], panel.at[k % 2], panel_sem.at[k % 2]
+            )
+
+        for k in range(2):
+            fetch(k).start()
+
+    def extra(k):
+        fetch(k).wait()
+        node = parent_ref[level_starts[lower] + k]
+        total = None
+        for at, upper in enumerate(uppers):
+            node = parent_ref[node]
+            split = SPLITS[upper]
+            slot = jnp.clip(node - level_starts[upper], 0, level_counts[upper] - 1) * split
+            value = jnp.concatenate([known[at][slot + half] for half in range(split)], axis=1)
+            product = lax.dot_general(
+                panel[k % 2, at], value, (((0,), (0,)), ((), ())), preferred_element_type=jnp.float32
+            )
+            total = product if total is None else total + product
+        partial_ref[k] = bf16(total)
+
+        @pl.when(k + 2 < level_counts[lower])
+        def _():
+            fetch(k + 2).start()
+
+    split = units // count
     load = pltpu.make_async_copy(diag_hbm.at[pl.ds(start, count)], diag, load_sem.at[0])
     load.start()
     enter(leaf, col)
@@ -432,7 +475,7 @@
             corrected = z_ref[k]
         else:
             corrected = y_ref[k]
-        part[k] = bf16(jnp.dot(diag[k // SPLIT], corrected, preferred_element_type=jnp.float32))
+        part[k] = bf16(jnp.dot(diag[k // split], corrected, preferred_element_type=jnp.float32))
         col.stage_start(k)
 
     stages = []
@@ -445,11 +488,17 @@
         ]
         lag = 2 * LAG + 1
     stages += [(lag, divide), (lag + LAG, col.stage_join), (lag + 2 * LAG, col.stage_sum)]
+
+    def finish(k):
+        col.stage_end(k)
+        col.drain(k)
+        if has_update:
+            leaf.drain(k)
+
+    stages.append((lag + 3 * LAG, finish))
+    if lower is not None:
+        stages.insert(0, (1, extra))
     staged(units, stages)
-    each(units, col.stage_end)
-    each(units, col.drain)
-    if has_update:
-        each(units, leaf.drain)
 
 
 def leaf_scratch(units, rows, width):
@@ -469,13 +518,14 @@
     start, count = level_starts[level], level_counts[level]
     depth, rows = diag.shape[1], diag.shape[2]
     rhs = right_side.shape[2]
-    units, width = count * SPLIT, rhs // SPLIT
+    split = SPLITS[level]
+    units, width = count * split, rhs // split
     has_update = update is not None
     block = pltpu.VMEM((units, depth, width), jnp.bfloat16)
     scratch = [
-        pltpu.VMEM((SPLIT, count, depth, width), jnp.float32),
+        pltpu.VMEM((split, count, depth, width), jnp.float32),
         pltpu.VMEM((count, depth, rows), jnp.bfloat16),
-        pltpu.SemaphoreType.DMA((SPLIT + 1,)),
+        pltpu.SemaphoreType.DMA((split + 1,)),
         pltpu.VMEM((units, rows, width), jnp.bfloat16),
     ]
     scratch += leaf_scratch(units, rows, width) + sem_scratch(units, 6)
@@ -497,7 +547,7 @@
     )(*([update] * has_update), right_side, diag)
 
 
-def backward_level(level, update, forward_value, diag):
+def backward_level(level, update, forward_value, diag, panels, solutions, parent):
     start, count = level_starts[level], level_counts[level]
     depth, rows = diag.shape[1], diag.shape[2]
     units, width = forward_value.shape[0], forward_value.shape[2]
@@ -510,35 +560,44 @@
         scratch += leaf_scratch(units, rows, width) + sem_scratch(units, 6)
     vmem = pl.BlockSpec(memory_space=pltpu.VMEM)
     anywhere = pl.BlockSpec(memory_space=pl.ANY)
-    return pl.pallas_call(
-        functools.partial(backward_kernel, start, count, has_update),
-        out_shape=jax.ShapeDtypeStruct((units, depth, width), jnp.bfloat16),
-        in_specs=[vmem] * has_update + [vmem, anywhere],
-        out_specs=vmem,
+    lower = level - 1 if 1 <= level <= 3 else None
+    uppers = list(range(level + 1, 5)) if lower is not None else []
+    out_shape = [jax.ShapeDtypeStruct((units, depth, width), jnp.bfloat16)]
+    extra_specs, extra_args = [], []
+    if lower is not None:
+        rhs = width * SPLITS[level]
+        out_shape.append(jax.ShapeDtypeStruct((level_counts[lower], rows, rhs), jnp.bfloat16))
+        extra_specs = [pl.BlockSpec(memory_space=pltpu.SMEM), anywhere] + [vmem] * len(uppers)
+        extra_args = [parent, panels] + [solutions[upper] for upper in uppers]
+        scratch += [
+            pltpu.VMEM((2, 3 - lower, depth, rows), jnp.bfloat16),
+            pltpu.SemaphoreType.DMA((2,)),
+        ]
+    outs = pl.pallas_call(
+        functools.partial(backward_kernel, start, count, units, has_update, lower, uppers),
+        out_shape=out_shape,
+        in_specs=[vmem] * has_update + [vmem, anywhere] + extra_specs,
+        out_specs=[vmem] * len(out_shape),
         scratch_shapes=scratch,
         name=f"backward_level_{level}",
         cost_estimate=cost(2 * units * rows * depth * width, 2 * count * rows * depth),
         compiler_params=pltpu.CompilerParams(
             collective_id=5 + level, has_side_effects=True, vmem_limit_bytes=VMEM_BYTES
         ),
-    )(*([update] * has_update), forward_value, diag)
-
-
-def climb(parent_ref, node, distance):
-    for _ in range(distance):
-        node = parent_ref[node]
-    return node
+    )(*([update] * has_update), forward_value, diag, *extra_args)
+    return outs[0], (outs[1] if lower is not None else None)
 
 
 def joined_columns(ref):
-    return jnp.concatenate([ref[half] for half in range(SPLIT)], axis=1)
+    return jnp.concatenate([ref[half] for half in range(ref.shape[0])], axis=1)
 
 
 def forward_update(level, panels, value, earlier, parent):
     count, start = level_counts[level], level_starts[level]
     rows, depth = panels.shape[1], panels.shape[2]
-    width = value.shape[2]
-    rhs = width * SPLIT
+    own, split = SPLITS[level], SPLITS[level + 1]
+    rhs = value.shape[2] * own
+    width = rhs // split
     distances = 4 - level
     base = pair_offset(level)
     above = level_counts[level + 1 :]
@@ -565,8 +624,8 @@
         @pl.when(k == count - 1)
         def _():
             for slot in range(above[0]):
-                for half in range(SPLIT):
-                    done[slot * SPLIT + half] = bf16(total[slot, :, half * width : (half + 1) * width])
+                for half in range(split):
+                    done[slot * split + half] = bf16(total[slot, :, half * width : (half + 1) * width])
 
     def panel_at(d):
         return lambda k, parent_ref: (base + k * distances + d, 0, 0)
@@ -579,12 +638,12 @@
             num_scalar_prefetch=1,
             grid=(count,),
             in_specs=[pl.BlockSpec((1, rows, depth), panel_at(d)) for d in range(distances)]
-            + [pl.BlockSpec((SPLIT, depth, width), lambda k, parent_ref: (k, 0, 0))]
+            + [pl.BlockSpec((own, depth, rhs // own), lambda k, parent_ref: (k, 0, 0))]
             + [whole(shape) for shape in shapes[: given]],
-            out_specs=[whole((above[0] * SPLIT, rows, width))] + [whole(shape) for shape in shapes[1:]],
+            out_specs=[whole((above[0] * split, rows, width))] + [whole(shape) for shape in shapes[1:]],
             scratch_shapes=[pltpu.VMEM(shapes[0], jnp.float32)],
         ),
-        out_shape=[jax.ShapeDtypeStruct((above[0] * SPLIT, rows, width), jnp.bfloat16)]
+        out_shape=[jax.ShapeDtypeStruct((above[0] * split, rows, width), jnp.bfloat16)]
         + [jax.ShapeDtypeStruct(shape, jnp.float32) for shape in shapes[1:]],
         name=f"forward_update_{level}",
         cost_estimate=cost(
@@ -595,73 +654,72 @@
     return outs[0], outs[1:]
 
 
-def backward_update(level, panels, solutions, parent):
+def backward_update(level, panels, solutions, partial, parent):
     count, start = level_counts[level], level_starts[level]
     rows, depth = panels.shape[1], panels.shape[2]
-    width = solutions[4].shape[2]
+    own, split = SPLITS[level + 1], SPLITS[level]
+    rhs = solutions[level + 1].shape[2] * own
+    width = rhs // split
     distances = 4 - level
     base = pair_offset(level)
-
-    def body(parent_ref, *refs):
-        total = None
-        for d in range(distances):
-            product = lax.dot_general(
-                refs[d][0],
-                joined_columns(refs[distances + d]),
-                (((0,), (0,)), ((), ())),
-                preferred_element_type=jnp.float32,
-            )
-            total = product if total is None else total + product
-        for half in range(SPLIT):
-            refs[2 * distances][half] = bf16(total[:, half * width : (half + 1) * width])
-
-    def panel_at(d):
-        return lambda k, parent_ref: (base + k * distances + d, 0, 0)
-
-    def upper_at(d):
-        first = level_starts[level + 1 + d]
-        return lambda k, parent_ref: (climb(parent_ref, start + k, d + 1) - first, 0, 0)
+    first = level_starts[level + 1]
+    given = partial is not None
+
+    def body(parent_ref, panel, upper, *refs):
+        total = lax.dot_general(
+            panel[0], joined_columns(upper), (((0,), (0,)), ((), ())), preferred_element_type=jnp.float32
+        )
+        if given:
+            total = total + f32(refs[0][0])
+        for half in range(split):
+            refs[-1][half] = bf16(total[:, half * width : (half + 1) * width])
 
     return pl.pallas_call(
         body,
         grid_spec=pltpu.PrefetchScalarGridSpec(
             num_scalar_prefetch=1,
             grid=(count,),
-            in_specs=[pl.BlockSpec((1, rows, depth), panel_at(d)) for d in range(distances)]
-            + [pl.BlockSpec((SPLIT, rows, width), upper_at(d)) for d in range(distances)],
-            out_specs=pl.BlockSpec((SPLIT, depth, width), lambda k, _: (k, 0, 0)),
+            in_specs=[
+                pl.BlockSpec((1, rows, depth), lambda k, parent_ref: (base + k * distances, 0, 0)),
+                pl.BlockSpec(
+                    (own, rows, rhs // own), lambda k, parent_ref: (parent_ref[start + k] - first, 0, 0)
+                ),
+            ]
+            + [pl.BlockSpec((1, depth, rhs), lambda k, parent_ref: (k, 0, 0))] * given,
+            out_specs=pl.BlockSpec((split, depth, width), lambda k, parent_ref: (k, 0, 0)),
         ),
-        out_shape=jax.ShapeDtypeStruct((count * SPLIT, depth, width), jnp.bfloat16),
+        out_shape=jax.ShapeDtypeStruct((count * split, depth, width), jnp.bfloat16),
         name=f"backward_update_{level}",
-        cost_estimate=cost(
-            2 * count * distances * rows * depth * width * SPLIT, 2 * count * distances * rows * depth
-        ),
+        cost_estimate=cost(2 * count * rows * depth * rhs, 2 * count * rows * depth),
         compiler_params=pltpu.CompilerParams(vmem_limit_bytes=VMEM_BYTES),
-    )(parent, *([panels] * distances), *[solutions[level + 1 + d] for d in range(distances)])
+    )(parent, panels, solutions[level + 1], *([partial] * given))
 
 
 def assemble(solutions, node_total):
-    rows, width = solutions[0].shape[1], solutions[0].shape[2]
+    rows = solutions[0].shape[1]
+    rhs = solutions[0].shape[2] * SPLITS[0]
 
     def body(*refs):
         out = refs[5]
         for level in range(5):
 
             def store(k, level=level):
-                for half in range(SPLIT):
+                split = SPLITS[level]
+                width = rhs // split
+                for half in range(split):
                     out[level_starts[level] + k, :, half * width : (half + 1) * width] = f32(
-                        refs[level][k * SPLIT + half]
+                        refs[level][k * split + half]
                     )
 
             each(level_counts[level], store)
 
     return pl.pallas_call(
         body,
-        out_shape=jax.ShapeDtypeStruct((node_total, rows, width * SPLIT), jnp.float32),
+        out_shape=jax.ShapeDtypeStruct((node_total, rows, rhs), jnp.float32),
         in_specs=[pl.BlockSpec(memory_space=pltpu.VMEM)] * 5,
         out_specs=pl.BlockSpec(memory_space=pltpu.VMEM),
         name="assemble",
-        cost_estimate=cost(0, node_total * rows * width * SPLIT * 6),
+        cost_estimate=cost(0, node_total * rows * rhs * 6),
         compiler_params=pltpu.CompilerParams(vmem_limit_bytes=VMEM_BYTES),
     )(*solutions)
 
@@ -674,9 +732,12 @@
         update, earlier = forward_update(level, panels, values[level], earlier, parent)
         values.append(forward_level(level + 1, update, right_side, diag))
     solutions = [None] * 5
+    partial = None
     for level in (4, 3, 2, 1, 0):
-        update = backward_update(level, panels, solutions, parent) if level < 4 else None
-        solutions[level] = backward_level(level, update, values[level], diag)
+        update = backward_update(level, panels, solutions, partial, parent) if level < 4 else None
+        solutions[level], partial = backward_level(
+            level, update, values[level], diag, panels, solutions, parent
+        )
     return assemble(solutions, right_side.shape[0])
 
 

time: 565 us -> 547 us (0.968)
  Pallas kernels: 563 us -> 546 us
    pallas_call x4, Pallas kernels: 42.9 us -> 32.7 us  [backward_update(): pl.pallas_call(body, grid_spec=pltpu.PrefetchScalarGridSpec(num_scalar_pr...]
    pallas_call x5, Pallas kernels: 231 us -> 225 us  [forward_level(): pl.pallas_call(functools.partial(forward_kernel, start, count, has_update...]
where the time goes in v3:
time: 547 us; the launch traced here: 546 us
  Pallas kernels  546 us (100%)
    pallas_call x5, Pallas kernels, backward_level(): pl.pallas_call(functools.partial(backward_kernel, start, count, units, ha...  239 us
    pallas_call x5, Pallas kernels, forward_level(): pl.pallas_call(functools.partial(forward_kernel, start, count, has_update...  225 us
    pallas_call x4, Pallas kernels, forward_update(): pl.pallas_call(body, grid_spec=pltpu.PrefetchScalarGridSpec(num_scalar_pr...  42.5 us
    pallas_call x4, Pallas kernels, backward_update(): pl.pallas_call(body, grid_spec=pltpu.PrefetchScalarGridSpec(num_scalar_pr...  32.7 us

profile of v3, /device:TPU:0, one launch (start us, length us, event | category | flops | bytes accessed | tf_op | source)
XLA Modules:
  0.0 545.6 jit_solution(15747210768701607804)
XLA Ops:
  0.0 72.1 %forward_level_0.1.refs_4_.refs_1_ = bf16[16,640,256]{2,1,0:T(8,128)(2,1)} custom-call(f32[31,320,256]{2,1,0:T(8,128)} %refs_1_.13, bf16[31,320,640]{2,1,0:T(8,128)(2,1)} %bitcast.1), custom_call_target="tpu_custom_call" | custom-call | flops 1677721600 | bytes 11796480 | tf_op jit(solution)/shard_map/forward_level_0/pallas_call | solution.py:536
  72.1 21.9 %forward_update_0.1 = (bf16[16,320,128]{2,1,0:T(8,128)(2,1)}, f32[4,320,256]{2,1,0:T(8,128)}, f32[2,320,256]{2,1,0:T(8,128)}, f32[1,320,256]{2,1,0:T(8,128)}) custom-call(s32[31]{0:T(128)} %parent_ref.15, bf16[98,320,640]{2,1,0:T(8,128)(2,1)} %panel.7, bf16[98,320,640]{2,1,0:T(8,128)(2,1)} %panel.7, bf16[98,320,640]{2,1,0:T(8,128)(2,1)} %panel.7, ...), custom_call_target="tpu_custom_call" | custom-call | flops 6710886400 | bytes 31457280 | tf_op jit(solution)/shard_map/forward_update_0/pallas_call | solution.py:635
  93.9 58.7 %forward_level_1.1.refs_3_.refs_1_ = bf16[16,640,128]{2,1,0:T(8,128)(2,1)} custom-call(bf16[16,320,128]{2,1,0:T(8,128)(2,1)} %get-tuple-element.20.refs_0_, f32[31,320,256]{2,1,0:T(8,128)} %refs_1_.13, bf16[31,320,640]{2,1,0:T(8,128)(2,1)} %bitcast.2), custom_call_target="tpu_custom_call" | custom-call | flops 838860800 | bytes 5898240 | tf_op jit(solution)/shard_map/forward_level_1/pallas_call | solution.py:536
  152.7 11.5 %forward_update_1.1 = (bf16[8,320,128]{2,1,0:T(8,128)(2,1)}, f32[2,320,256]{2,1,0:T(8,128)}, f32[1,320,256]{2,1,0:T(8,128)}) custom-call(s32[31]{0:T(128)} %parent_ref.15, bf16[98,320,640]{2,1,0:T(8,128)(2,1)} %panel.7, bf16[98,320,640]{2,1,0:T(8,128)(2,1)} %panel.7, bf16[98,320,640]{2,1,0:T(8,128)(2,1)} %panel.7, ...), custom_call_target="tpu_custom_call" | custom-call | flops 2516582400 | bytes 12451840 | tf_op jit(solution)/shard_map/forward_update_1/pallas_call | solution.py:635
  164.2 38.6 %forward_level_2.1.refs_2_.refs_1_ = bf16[8,640,128]{2,1,0:T(8,128)(2,1)} custom-call(bf16[8,320,128]{2,1,0:T(8,128)(2,1)} %get-tuple-element.24.refs_0_, f32[31,320,256]{2,1,0:T(8,128)} %refs_1_.13, bf16[31,320,640]{2,1,0:T(8,128)(2,1)} %bitcast.3), custom_call_target="tpu_custom_call" | custom-call | flops 419430400 | bytes 2949120 | tf_op jit(solution)/shard_map/forward_level_2/pallas_call | solution.py:536
  202.8 5.9 %forward_update_2.1 = (bf16[4,320,128]{2,1,0:T(8,128)(2,1)}, f32[1,320,256]{2,1,0:T(8,128)}) custom-call(s32[31]{0:T(128)} %parent_ref.15, bf16[98,320,640]{2,1,0:T(8,128)(2,1)} %panel.7, bf16[98,320,640]{2,1,0:T(8,128)(2,1)} %panel.7, bf16[8,640,128]{2,1,0:T(8,128)(2,1)} %forward_level_2.1.refs_2_.refs_1_, f32[2,320,256]{2,1,0:T(8,128)} %get-tuple-element.25.refs_3_, ...), custom_call_target="tpu_custom_call" | custom-call | flops 838860800 | bytes 4587520 | tf_op jit(solution)/shard_map/forward_update_2/pallas_call | solution.py:635
  208.7 29.9 %forward_level_3.1.refs_1_ = bf16[4,640,128]{2,1,0:T(8,128)(2,1)} custom-call(bf16[4,320,128]{2,1,0:T(8,128)(2,1)} %get-tuple-element.27.refs_0_, f32[31,320,256]{2,1,0:T(8,128)} %refs_1_.13, bf16[31,320,640]{2,1,0:T(8,128)(2,1)} %bitcast.4), custom_call_target="tpu_custom_call" | custom-call | flops 209715200 | bytes 1474560 | tf_op jit(solution)/shard_map/forward_level_3/pallas_call | solution.py:536
  238.6 3.2 forward_update_3.1.refs_0_
  241.9 25.2 %forward_level_4.1.refs_0_ = bf16[2,640,128]{2,1,0:T(8,128)(2,1)} custom-call(bf16[2,320,128]{2,1,0:T(8,128)(2,1)} %forward_update_3.1.refs_0_, f32[31,320,256]{2,1,0:T(8,128)} %refs_1_.13, bf16[31,320,640]{2,1,0:T(8,128)(2,1)} %bitcast.5), custom_call_target="tpu_custom_call" | custom-call | flops 104857600 | bytes 737280 | tf_op jit(solution)/shard_map/forward_level_4/pallas_call | solution.py:536
  267.1 16.3 %backward_level_4.1.upper.refs_5_.refs_6_.refs_7_.refs_4_ = bf16[2,320,128]{2,1,0:T(8,128)(2,1)} custom-call(bf16[2,640,128]{2,1,0:T(8,128)(2,1)} %forward_level_4.1.refs_0_, bf16[31,320,640]{2,1,0:T(8,128)(2,1)} %bitcast.6), custom_call_target="tpu_custom_call" | custom-call | flops 104857600 | bytes 409600 | tf_op jit(solution)/shard_map/backward_level_4/pallas_call | solution.py:576
  283.4 3.2 backward_update_3.1.refs_0_
  286.6 29.7 %backward_level_3.1 = (bf16[4,320,128]{2,1,0:T(8,128)(2,1)}, bf16[4,640,256]{2,1,0:T(8,128)(2,1)}) custom-call(bf16[4,640,128]{2,1,0:T(8,128)(2,1)} %backward_update_3.1.refs_0_, bf16[4,640,128]{2,1,0:T(8,128)(2,1)} %forward_level_3.1.refs_1_, bf16[31,320,640]{2,1,0:T(8,128)(2,1)} %bitcast.7, s32[31]{0:T(128)} %parent_ref.15, bf16[98,320,640]{2,1,0:T(8,128)(2,1)} %panel.7, ...), custom_call_target="tpu_custom_call" | custom-call | flops 209715200 | bytes 819200 | tf_op jit(solution)/shard_map/backward_level_3/pallas_call | solution.py:576
  316.4 5.3 backward_update_2.1.refs_0_
  321.6 40.6 %backward_level_2.1 = (bf16[8,320,128]{2,1,0:T(8,128)(2,1)}, bf16[8,640,256]{2,1,0:T(8,128)(2,1)}) custom-call(bf16[8,640,128]{2,1,0:T(8,128)(2,1)} %backward_update_2.1.refs_0_, bf16[8,640,128]{2,1,0:T(8,128)(2,1)} %forward_level_2.1.refs_2_.refs_1_, bf16[31,320,640]{2,1,0:T(8,128)(2,1)} %bitcast.8, s32[31]{0:T(128)} %parent_ref.15, ...), custom_call_target="tpu_custom_call" | custom-call | flops 419430400 | bytes 1638400 | tf_op jit(solution)/shard_map/backward_level_2/pallas_call | solution.py:576
  362.2 8.7 %backward_update_1.1.refs_0_ = bf16[16,640,128]{2,1,0:T(8,128)(2,1)} custom-call(s32[31]{0:T(128)} %parent_ref.15, bf16[98,320,640]{2,1,0:T(8,128)(2,1)} %panel.7, bf16[8,320,128]{2,1,0:T(8,128)(2,1)} %get-tuple-element.31.upper.refs_5_.refs_2_, bf16[8,640,256]{2,1,0:T(8,128)(2,1)} %get-tuple-element.32.refs_0_), custom_call_target="tpu_custom_call" | custom-call | flops 838860800 | bytes 3276800 | tf_op jit(solution)/shard_map/backward_update_1/pallas_call | solution.py:677
  370.9 60.1 %backward_level_1.1 = (bf16[16,320,128]{2,1,0:T(8,128)(2,1)}, bf16[16,640,256]{2,1,0:T(8,128)(2,1)}) custom-call(bf16[16,640,128]{2,1,0:T(8,128)(2,1)} %backward_update_1.1.refs_0_, bf16[16,640,128]{2,1,0:T(8,128)(2,1)} %forward_level_1.1.refs_3_.refs_1_, bf16[31,320,640]{2,1,0:T(8,128)(2,1)} %bitcast.9, s32[31]{0:T(128)} %parent_ref.15, ...), custom_call_target="tpu_custom_call" | custom-call | flops 838860800 | bytes 3276800 | tf_op jit(solution)/shard_map/backward_level_1/pallas_call | solution.py:576
  431.1 15.5 %backward_update_0.1.refs_0_ = bf16[16,640,256]{2,1,0:T(8,128)(2,1)} custom-call(s32[31]{0:T(128)} %parent_ref.15, bf16[98,320,640]{2,1,0:T(8,128)(2,1)} %panel.7, bf16[16,320,128]{2,1,0:T(8,128)(2,1)} %get-tuple-element.33.upper.refs_1_, bf16[16,640,256]{2,1,0:T(8,128)(2,1)} %get-tuple-element.34.refs_0_), custom_call_target="tpu_custom_call" | custom-call | flops 1677721600 | bytes 6553600 | tf_op jit(solution)/shard_map/backward_update_0/pallas_call | solution.py:677
  446.5 92.0 %backward_level_0.1.refs_0_ = bf16[16,320,256]{2,1,0:T(8,128)(2,1)} custom-call(bf16[16,640,256]{2,1,0:T(8,128)(2,1)} %backward_update_0.1.refs_0_, bf16[16,640,256]{2,1,0:T(8,128)(2,1)} %forward_level_0.1.refs_4_.refs_1_, bf16[31,320,640]{2,1,0:T(8,128)(2,1)} %bitcast.10), custom_call_target="tpu_custom_call" | custom-call | flops 1677721600 | bytes 6553600 | tf_op jit(solution)/shard_map/backward_level_0/pallas_call | solution.py:576
  538.5 7.1 %assemble.1 = f32[31,320,256]{2,1,0:T(8,128)} custom-call(bf16[16,320,256]{2,1,0:T(8,128)(2,1)} %backward_level_0.1.refs_0_, bf16[16,320,128]{2,1,0:T(8,128)(2,1)} %get-tuple-element.33.upper.refs_1_, bf16[8,320,128]{2,1,0:T(8,128)(2,1)} %get-tuple-element.31.upper.refs_5_.refs_2_, bf16[4,320,128]{2,1,0:T(8,128)(2,1)} %get-tuple-element.29.upper.refs_5_.refs_6_.refs_3_, ...), custom_call_target="tpu_custom_call" | custom-call | bytes 15237120 | tf_op jit(solution)/shard_map/assemble/pallas_call | solution.py:716
